TPU v7x, 32 devices: a whole 2x2x4 slice. The times are simulated.
32 devices in a mesh: trainer: 8 (over y, x, core), depth: 4 (over z).
Axes of the slice: x: 2, y: 2, z: 4, core: 2. Of those that a mesh axis runs over, the one named last changes fastest.
Arguments:
- latent: bfloat16 [8, 8, 16, 16, 256], P('trainer', 'depth'), may hold values from -6 to 6
- gen_first: float32 [8, 256, 8192], P('trainer', 'depth'), may hold values from -0.125 to 0.125
- gen_second: float32 [8, 128, 4096], P('trainer', 'depth'), may hold values from -0.1875 to 0.1875
- critic: bfloat16 [8, 4096, 128], P('trainer'), may hold values from -0.09375 to 0.09375
- partner: int32 [8], replicated, may hold values from 0 to 7, as said below
Outputs:
- judged: bfloat16 [8, 2, 16, 32, 32, 128], P('trainer', None, 'depth')
Inputs may be any that keep to these rules, and one draw needn't show every extreme that they name: partner[t] = t XOR m for every t, with one m for the whole array, 1 <= m < 8; so partner[partner[t]] = t and no trainer is its own partner.
All inputs are finite; a program needn't handle non-finite values.
Results may differ from a plain program's by a relative error of at most 0.0071.
Values may be sent and summed in bfloat16 or wider, within the bound.
A program may use at most 128 MiB of HBM per device.

v0:
```python
import jax
import jax.numpy as jnp
from jax import lax
from jax.sharding import PartitionSpec as P

leak_slope = 0.2
layout = ("NDHWC", "DHWIO", "NDHWC")


def for_sending(value):

    def short(part):
        return part.astype(jnp.bfloat16) if part.dtype == jnp.float32 else part

    return jax.tree.map(short, value)


def partner_2(value, axis, distance):
    mask = 2**distance
    pairs = [(source, source ^ mask) for source in range(lax.axis_size(axis))]
    return lax.ppermute(value, axis, pairs)


def extended(block, sides, width):
    for axis, dim in sides:
        count = lax.axis_size(axis)
        forward = [(i, i + 1) for i in range(count - 1)]
        backward = [(target, source) for source, target in forward]
        low = lax.ppermute(
            lax.slice_in_dim(block, block.shape[dim] - width, None, axis=dim), axis, forward
        )
        high = lax.ppermute(lax.slice_in_dim(block, 0, width, axis=dim), axis, backward)
        block = jnp.concatenate([low, block, high], axis=dim)
    return block


def alternate(blocks):
    stacked = jnp.stack(
        [jnp.stack([jnp.stack(pair_w, 0) for pair_w in pair_h], 0) for pair_h in blocks], 0
    )
    planes, height, across, channels = blocks[0][0][0].shape
    reordered = jnp.transpose(stacked, (3, 0, 4, 1, 5, 2, 6))
    return reordered.reshape(2 * planes, 2 * height, 2 * across, channels)


def transposed(volume, kernel):
    planes = volume.shape[0] - 2
    height = volume.shape[1]
    across = volume.shape[2]
    padded = jnp.pad(volume, ((0, 0), (1, 1), (1, 1), (0, 0)))
    flipped = jnp.flip(kernel, (0, 1, 2))
    blocks = []
    for along_depth in (0, 1):
        height_blocks = []
        for along_height in (0, 1):
            width_blocks = []
            for along_width in (0, 1):
                window = padded[
                    along_depth : along_depth + planes + 1,
                    along_height : along_height + height + 1,
                    along_width : along_width + across + 1,
                ]
                kernel_taps = flipped[along_depth::2, along_height::2, along_width::2]
                result = lax.conv_general_dilated(
                    window[None],
                    kernel_taps,
                    (1, 1, 1),
                    "VALID",
                    dimension_numbers=layout,
                    preferred_element_type=jnp.float32,
                )
                width_blocks.append(result[0])
            height_blocks.append(width_blocks)
        blocks.append(height_blocks)
    return alternate(blocks)


def strided(volume, kernel):
    result = lax.conv_general_dilated(
        volume[None],
        kernel,
        (2, 2, 2),
        ((0, 0), (1, 1), (1, 1)),
        dimension_numbers=layout,
        preferred_element_type=jnp.float32,
    )
    return result[0]


def judge(density, critic_kernel):
    scored = strided(density, critic_kernel)
    return jnp.where(scored > 0, scored, leak_slope * scored).astype(jnp.bfloat16)


def unfold(weight):
    in_channels = weight.shape[0]
    shaped = weight.reshape(in_channels, 4, 4, 4, weight.shape[1] // 64)
    return jnp.transpose(shaped, (1, 2, 3, 0, 4))


def swap_bits(values, offset, rounds):
    for bit_number in range(rounds):
        moved_values = jax.tree.map(
            lambda part, own: part.astype(own.dtype),
            partner_2(for_sending(values), "trainer", bit_number),
            values,
        )
        chosen = jnp.bitwise_and(jnp.right_shift(offset, bit_number), 1) == 1
        values = jax.tree.map(
            lambda moved, kept: jnp.where(chosen, moved, kept), moved_values, values
        )
    return values


def every_layer(seed_planes, first_kernel, second_kernel):
    hidden = jnp.maximum(transposed(seed_planes, first_kernel), 0.0).astype(jnp.bfloat16)
    hidden = extended(hidden, (("depth", 0),), 1)
    density = jnp.tanh(transposed(hidden, second_kernel)).astype(jnp.bfloat16)
    return extended(density, (("depth", 0),), 1)


def local(latent, gen_first, gen_second, critic, partner):
    trainer_index = lax.axis_index("trainer")
    offset = jnp.bitwise_xor(partner[trainer_index], trainer_index)
    rounds = lax.axis_size("trainer").bit_length() - 1
    first_shard = gen_first[0].astype(jnp.bfloat16)
    second_shard = gen_second[0].astype(jnp.bfloat16)
    mate_first_shard, mate_second_shard = swap_bits((first_shard, second_shard), offset, rounds)
    own_first, own_second = (
        lax.all_gather(first_shard, "depth", axis=0, tiled=True),
        lax.all_gather(second_shard, "depth", axis=0, tiled=True),
    )
    mate_first, mate_second = (
        lax.all_gather(mate_first_shard, "depth", axis=0, tiled=True),
        lax.all_gather(mate_second_shard, "depth", axis=0, tiled=True),
    )
    seed_planes = extended(latent[0], (("depth", 0),), 1)
    critic_kernel = critic[0].reshape(4, 4, 4, critic.shape[1] // 64, critic.shape[2])
    own_density = every_layer(seed_planes, unfold(own_first), unfold(own_second))
    mate_density = every_layer(seed_planes, unfold(mate_first), unfold(mate_second))
    return jnp.stack([judge(own_density, critic_kernel), judge(mate_density, critic_kernel)])[None]


def solution(mesh):
    in_specs = (
        P("trainer", "depth", None, None, None),
        P("trainer", "depth", None),
        P("trainer", "depth", None),
        P("trainer", None, None),
        P(),
    )
    out_specs = P("trainer", None, "depth", None, None, None)
    return jax.shard_map(local, mesh=mesh, in_specs=in_specs, out_specs=out_specs, check_vma=False)
```

profile of v0, /device:TPU:0, one launch (start us, length us, event | category | flops | bytes accessed | tf_op | source)
XLA Modules:
  0.0 547.3 jit_solution(16959260514625677894)
XLA Ops:
  15.8 5.1 collective-permute-done.12
  24.3 6.4 %collective-permute-done.13 = bf16[32,4096]{1,0:T(8,128)(2,1)S(1)} collective-permute-done((bf16[32,4096]{1,0:T(8,128)(2,1)}, bf16[32,4096]{1,0:T(8,128)(2,1)S(1)}, u32[]{:S(2)}, u32[]{:S(2)}) %collective-permute-start.13) | collective-permute-done | bytes 262176 | tf_op jit(solution)/shard_map/ppermute | solution.py:21
  38.3 3.5 collective-permute-start
  44.5 4.1 collective-permute-done.1
  69.6 3.7 all-gather.9.cloned.1.call-done
  75.5 79.6 %all-gather.11.cloned.1.call-done = bf16[1,256,8192]{2,1,0:T(8,128)(2,1)} async-done(((bf16[1,64,8192]{2,1,0:T(8,128)(2,1)}), bf16[1,256,8192]{2,1,0:T(8,128)(2,1)}) %all-gather.11.cloned.1.call-update) | async-done | bytes 4194320 | tf_op jit(solution)/shard_map/all_gather | solution.py:130
  155.1 6.4 %copy.124 = bf16[1,256,8192]{1,2,0:T(8,128)(2,1)} copy(bf16[1,256,8192]{2,1,0:T(8,128)(2,1)} %all-gather.11.cloned.1.call-done) | data formatting | bytes 8388608 | tf_op jit(solution)/shard_map/all_gather | solution.py:130
  161.5 7.3 %copy.125 = bf16[256,4,4,4,128]{4,0,3,2,1:T(8,128)(2,1)} copy(bf16[256,4,4,4,128]{0,4,3,2,1:T(8,128)(2,1)} %bitcast.423) | data formatting | bytes 8388608 | tf_op jit(solution)/shard_map/reshape | solution.py:97
  189.2 4.2 collective-permute-done.3
  196.0 4.2 slice_bitcast_fusion.31
  213.7 2.9 fusion.200
  223.7 3.3 fusion.206
  243.5 3.3 maximum_bitcast_fusion.3
  246.8 4.6 fusion.15
  251.4 14.7 %copy.182 = bf16[4,2,32,2,32,2,64]{6,5,4,3,2,1,0:T(2,128)(2,1)S(1)} copy(bf16[4,2,32,2,32,2,64]{6,2,4,0,5,3,1:T(8,128)(2,1)} %fusion.15) | data formatting | bytes 8388608 | tf_op jit(solution)/shard_map/convert_element_type | solution.py:118
  266.2 3.3 copy-done.1
  271.0 3.7 collective-permute-start.4
  276.0 6.4 %copy.187 = bf16[256,8192]{0,1:T(8,128)(2,1)} copy(bf16[256,8192]{1,0:T(8,128)(2,1)} %all-gather.7.cloned.1.call-done) | data formatting | bytes 8388608 | tf_op jit(solution)/shard_map/all_gather | solution.py:134
  282.4 7.3 %copy.188 = bf16[256,4,4,4,128]{4,0,3,2,1:T(8,128)(2,1)} copy(bf16[256,4,4,4,128]{0,4,3,2,1:T(8,128)(2,1)} %bitcast.424) | data formatting | bytes 8388608 | tf_op jit(solution)/shard_map/reshape | solution.py:97
  302.8 5.2 collective-permute-start.9
  309.4 6.9 %maximum_bitcast_fusion = bf16[10,64,1,64,64]{4,3,1,0,2:T(8,128)(2,1)} fusion(bf16[1,64,64,64]{3,2,1,0:T(8,128)(2,1)} %collective-permute-done.5, bf16[8,64,64,64]{3,2,1,0:T(8,128)(2,1)S(1)} %bitcast.420, bf16[1,64,64,64]{3,2,1,0:T(8,128)(2,1)S(1)} %collective-permute-done.4), kind=kLoop, calls=%fused_computation.13 | loop fusion | flops 5242880 | bytes 10485760 | tf_op jit(solution)/shard_map/broadcast_in_dim | solution.py:80
  316.3 15.4 %copy.245 = bf16[10,64,1,64,64]{4,1,3,0,2:T(8,128)(2,1)} copy(bf16[10,64,1,64,64]{4,3,1,0,2:T(8,128)(2,1)} %maximum_bitcast_fusion) | data formatting | bytes 10485760
  331.7 7.3 %pad.47.clone = bf16[10,64,1,80,64]{4,1,3,0,2:T(8,128)(2,1)S(1)} pad(bf16[10,64,1,64,64]{4,1,3,0,2:T(8,128)(2,1)} %copy.245, bf16[]{:T(256)} %constant.3.clone.1), padding=0_0x0_0x0_0x1_15x0_0 | pad | bytes 11796482 | tf_op jit(solution)/shard_map/broadcast_in_dim | solution.py:80
  339.0 9.4 %copy.185 = bf16[10,64,1,8,10,64]{5,3,4,1,0,2:T(8,128)(2,1)S(1)} copy(bf16[10,64,1,8,10,64]{5,1,4,3,0,2:T(8,128)(2,1)S(1)} %bitcast.416) | data formatting | bytes 13107200 | tf_op jit(solution)/shard_map/conv_general_dilated | solution.py:79
  348.4 3.5 slice.432
  357.0 3.9 slice_bitcast_fusion.23
  361.8 3.8 fusion.188
  367.2 3.8 fusion.170
  373.9 3.8 fusion.173
  379.3 3.8 fusion.176
  384.7 3.8 fusion.179
  390.0 3.8 fusion.182
  395.4 3.8 fusion.185
  400.8 3.8 fusion.167
  409.7 4.9 maximum_bitcast_fusion.13
  414.6 3.3 maximum_bitcast_fusion.5
  417.9 4.5 fusion.14
  422.4 14.7 %copy.231 = bf16[4,2,32,2,32,2,64]{6,5,4,3,2,1,0:T(2,128)(2,1)S(1)} copy(bf16[4,2,32,2,32,2,64]{6,2,4,0,5,3,1:T(8,128)(2,1)} %fusion.14) | data formatting | bytes 8388608 | tf_op jit(solution)/shard_map/convert_element_type | solution.py:118
  437.2 3.3 copy-done.2
  442.0 5.6 %collective-permute-start.14 = (bf16[1,64,64,64]{3,2,1,0:T(8,128)(2,1)}, bf16[1,64,64,64]{3,2,1,0:T(8,128)(2,1)}, u32[]{:S(2)}, u32[]{:S(2)}) collective-permute-start(bf16[1,64,64,64]{3,2,1,0:T(8,128)(2,1)} %get-tuple-element.7), channel_id=1, source_target_pairs={{0,1},{1,2},{2,3},{4,5},{5,6},{6,7},{8,9},{9,10},{10,11},{12,13},{... | collective-permute-start | bytes 1572872 | tf_op jit(solution)/shard_map/ppermute | solution.py:29
  448.9 15.4 %fusion.35 = bf16[4,32,8,5,128]{4,2,3,1,0:T(8,128)(2,1)} fusion(bf16[4,4,4,64,128]{4,3,2,1,0:T(8,128)(2,1)S(1)} %bitcast.413, bf16[10,64,1,7,3,64]{5,3,4,1,0,2:T(8,128)(2,1)S(1)} %copy-done.8, bf16[10,64,1,8,10,64]{5,3,4,1,0,2:T(8,128)(2,1)} %copy-done.3, pred[8,5]{0,1:T(8,128)(4,1)S(1)} %copy-done.56), kind=kOutput, calls=%fused_computation.61 | convolution fusion | flops 5313658880 | bytes 10633256 | tf_op jit(solution)/shard_map/conv_general_dilated | solution.py:79
  467.0 5.1 collective-permute-done.15
  472.1 10.7 %maximum_bitcast_fusion.1 = bf16[10,64,1,64,64]{4,3,1,0,2:T(8,128)(2,1)} fusion(bf16[1,64,64,64]{3,2,1,0:T(8,128)(2,1)} %collective-permute-done.15, bf16[8,64,64,64]{3,2,1,0:T(8,128)(2,1)} %bitcast.422, bf16[1,64,64,64]{3,2,1,0:T(8,128)(2,1)} %collective-permute-done.14), kind=kLoop, calls=%fused_computation.14 | loop fusion | flops 5242880 | bytes 10485760 | tf_op jit(solution)/shard_map/broadcast_in_dim | solution.py:80
  482.8 15.4 %copy.254 = bf16[10,64,1,64,64]{4,1,3,0,2:T(8,128)(2,1)} copy(bf16[10,64,1,64,64]{4,3,1,0,2:T(8,128)(2,1)} %maximum_bitcast_fusion.1) | data formatting | bytes 10485760
  498.2 7.3 %pad.81.clone = bf16[10,64,1,80,64]{4,1,3,0,2:T(8,128)(2,1)S(1)} pad(bf16[10,64,1,64,64]{4,1,3,0,2:T(8,128)(2,1)} %copy.254, bf16[]{:T(256)} %constant.3.clone.1), padding=0_0x0_0x0_0x1_15x0_0 | pad | bytes 11796482 | tf_op jit(solution)/shard_map/broadcast_in_dim | solution.py:80
  505.5 9.4 %copy.234 = bf16[10,64,1,8,10,64]{5,3,4,1,0,2:T(8,128)(2,1)S(1)} copy(bf16[10,64,1,8,10,64]{5,1,4,3,0,2:T(8,128)(2,1)S(1)} %bitcast.415) | data formatting | bytes 13107200 | tf_op jit(solution)/shard_map/conv_general_dilated | solution.py:79
  514.9 4.7 copy-done.4
  522.5 15.0 %fusion.36 = bf16[4,32,8,5,128]{4,2,3,1,0:T(8,128)(2,1)S(1)} fusion(bf16[4,4,4,64,128]{4,3,2,1,0:T(8,128)(2,1)S(1)} %bitcast.414, bf16[10,64,1,7,3,64]{5,3,4,1,0,2:T(8,128)(2,1)} %slice.470, bf16[10,64,1,8,10,64]{5,3,4,1,0,2:T(8,128)(2,1)} %copy-done.4, pred[8,5]{0,1:T(8,128)(4,1)S(1)} %copy-done.56), kind=kOutput, calls=%fused_computation.62 | convolution fusion | flops 5313658880 | bytes 10633256 | tf_op jit(solution)/shard_map/conv_general_dilated | solution.py:79
  (379 shorter events, 155.6 us)
Async XLA Ops:
  6.5 442.3 %copy-start = (bf16[1,4096,128]{2,1,0:T(8,128)(2,1)S(1)}, bf16[1,4096,128]{2,1,0:T(8,128)(2,1)}, u32[]{:S(2)}) copy-start(bf16[1,4096,128]{2,1,0:T(8,128)(2,1)} %param.8) | copy-start | bytes 3145732
  6.5 57.6 %all-gather.13.cloned.1.call-start = ((), (), s32[]{:S(2)}) async-start(), calls=%async_computation.3 | async-start | bytes 1310720 | tf_op jit(solution)/shard_map/all_gather | solution.py:131
  7.7 23.8 %copy-start.5 = (f32[1,64,8192]{2,1,0:T(8,128)S(1)}, f32[1,64,8192]{2,1,0:T(8,128)}, u32[]{:S(2)}) copy-start(f32[1,64,8192]{2,1,0:T(8,128)} %param.6) | copy-start | bytes 6291460
  7.7 2.5 collective-permute-start.11
  11.3 9.5 %collective-permute-start.12 = (bf16[32,4096]{1,0:T(8,128)(2,1)S(1)}, bf16[32,4096]{1,0:T(8,128)(2,1)}, u32[]{:S(2)}, u32[]{:S(2)}) collective-permute-start(bf16[32,4096]{1,0:T(8,128)(2,1)S(1)} %broadcast_select_fusion.3), channel_id=1, source_target_pairs={{0,8},{4,12},{8,0},{12,4},{16,24},{20,28},{24,16},{28,20},{1,9},{5... | collective-permute-start | bytes 786440 | tf_op jit(solution)/shard_map/ppermute | solution.py:21
  15.7 57.6 %all-gather.9.cloned.1.call-start = ((), (), s32[]{:S(2)}) async-start(), calls=%async_computation.1 | async-start | bytes 1310720 | tf_op jit(solution)/shard_map/all_gather | solution.py:135
  22.5 8.2 %collective-permute-start.13 = (bf16[32,4096]{1,0:T(8,128)(2,1)}, bf16[32,4096]{1,0:T(8,128)(2,1)S(1)}, u32[]{:S(2)}, u32[]{:S(2)}) collective-permute-start(bf16[32,4096]{1,0:T(8,128)(2,1)} %broadcast_select_fusion.4), channel_id=1, source_target_pairs={{0,16},{4,20},{8,24},{12,28},{16,0},{20,4},{24,8},{28,12},{1,17},{... | collective-permute-start | bytes 786440 | tf_op jit(solution)/shard_map/ppermute | solution.py:21
  31.5 123.7 %all-gather.11.cloned.1.call-start = ((), (), s32[]{:S(2)}) async-start(), calls=%async_computation.2 | async-start | bytes 5242880 | tf_op jit(solution)/shard_map/all_gather | solution.py:130
  32.6 243.3 %all-gather.7.cloned.1.call-start = ((), (), s32[]{:S(2)}) async-start(), calls=%async_computation | async-start | bytes 5242880 | tf_op jit(solution)/shard_map/all_gather | solution.py:134
  32.8 5.5 copy-start.40
  32.8 2.7 collective-permute-start.6
  36.8 29.9 %collective-permute-start.7 = (bf16[64,8192]{1,0:T(8,128)(2,1)}, bf16[64,8192]{1,0:T(8,128)(2,1)}, u32[]{:S(2)}, u32[]{:S(2)}) collective-permute-start(bf16[64,8192]{1,0:T(8,128)(2,1)} %broadcast_select_fusion), channel_id=1, source_target_pairs={{0,8},{4,12},{8,0},{12,4},{16,24},{20,28},{24,16},{28,20},{1,9},{5... | collective-permute-start | bytes 3145736 | tf_op jit(solution)/shard_map/ppermute | solution.py:21
  38.3 6.2 %collective-permute-start = (bf16[1,16,16,256]{3,2,1,0:T(8,128)(2,1)S(1)}, bf16[1,16,16,256]{3,2,1,0:T(8,128)(2,1)S(1)}, u32[]{:S(2)}, u32[]{:S(2)}) collective-permute-start(bf16[1,16,16,256]{3,2,1,0:T(8,128)(2,1)S(1)} %get-tuple-element.37), channel_id=1, source_target_pairs={{0,1},{1,2},{2,3},{4,5},{5,6},{6,7},{8,9},{9,10},{10,11},{12,13},{... | collective-permute-start | bytes 393224 | tf_op jit(solution)/shard_map/ppermute | solution.py:29
  41.8 6.9 %collective-permute-start.1 = (bf16[1,16,16,256]{3,2,1,0:T(8,128)(2,1)S(1)}, bf16[1,16,16,256]{3,2,1,0:T(8,128)(2,1)S(1)}, u32[]{:S(2)}, u32[]{:S(2)}) collective-permute-start(bf16[1,16,16,256]{3,2,1,0:T(8,128)(2,1)S(1)} %get-tuple-element.38), channel_id=1, source_target_pairs={{1,0},{2,1},{3,2},{5,4},{6,5},{7,6},{9,8},{10,9},{11,10},{13,12},{... | collective-permute-start | bytes 393224 | tf_op jit(solution)/shard_map/ppermute | solution.py:32
  52.0 1.2 copy-start.14
  52.9 115.9 %copy-start.41 = (bf16[3,17,1,7,1,256]{5,3,4,1,0,2:T(8,128)(2,1)}, bf16[3,17,1,7,1,256]{5,3,4,1,0,2:T(8,128)(2,1)S(1)}, u32[]{:S(2)}) copy-start(bf16[3,17,1,7,1,256]{5,3,4,1,0,2:T(8,128)(2,1)S(1)} %slice.381) | copy-start | bytes 548356
  53.5 1.1 copy-start.13
  55.0 1.1 copy-start.12
  56.5 1.1 copy-start.11
  58.0 1.1 copy-start.10
  59.5 1.1 copy-start.9
  68.0 116.4 %collective-permute-start.8 = (bf16[64,8192]{1,0:T(8,128)(2,1)S(1)}, bf16[64,8192]{1,0:T(8,128)(2,1)}, u32[]{:S(2)}, u32[]{:S(2)}) collective-permute-start(bf16[64,8192]{1,0:T(8,128)(2,1)S(1)} %broadcast_select_fusion.1), channel_id=1, source_target_pairs={{0,16},{4,20},{8,24},{12,28},{16,0},{20,4},{24,8},{28,12},{1,17},{... | collective-permute-start | bytes 3145736 | tf_op jit(solution)/shard_map/ppermute | solution.py:21
  161.5 7.4 %copy-start.16 = (bf16[3,17,1,8,3,256]{5,3,4,1,0,2:T(8,128)(2,1)S(1)}, bf16[3,17,1,8,3,256]{5,3,4,1,0,2:T(8,128)(2,1)}, u32[]{:S(2)}) copy-start(bf16[3,17,1,8,3,256]{5,3,4,1,0,2:T(8,128)(2,1)} %copy-done.15) | copy-start | bytes 1880068
  161.5 7.4 %copy-start.57 = (pred[8,3]{0,1:T(4,128)(4,1)S(1)}, pred[8,3]{0,1:T(4,128)(4,1)}, u32[]{:S(2)}) copy-start(pred[8,3]{0,1:T(4,128)(4,1)} %constant.168) | copy-start | bytes 76
  161.5 9.6 %copy-start.42 = (bf16[3,17,1,7,1,256]{5,3,4,1,0,2:T(8,128)(2,1)S(1)}, bf16[3,17,1,7,1,256]{5,3,4,1,0,2:T(8,128)(2,1)}, u32[]{:S(2)}) copy-start(bf16[3,17,1,7,1,256]{5,3,4,1,0,2:T(8,128)(2,1)} %slice.399) | copy-start | bytes 548356
  168.9 2.3 copy-start.7
  168.9 2.5 copy-start.19
  181.7 7.4 %collective-permute-start.2 = (bf16[1,32,32,128]{3,2,1,0:T(8,128)(2,1)}, bf16[1,32,32,128]{3,2,1,0:T(8,128)(2,1)S(1)}, u32[]{:S(2)}, u32[]{:S(2)}) collective-permute-start(bf16[1,32,32,128]{3,2,1,0:T(8,128)(2,1)} %get-tuple-element.25), channel_id=1, source_target_pairs={{0,1},{1,2},{2,3},{4,5},{5,6},{6,7},{8,9},{9,10},{10,11},{12,13},{... | collective-permute-start | bytes 786440 | tf_op jit(solution)/shard_map/ppermute | solution.py:29
  183.0 10.4 %collective-permute-start.3 = (bf16[1,32,32,128]{3,2,1,0:T(8,128)(2,1)}, bf16[1,32,32,128]{3,2,1,0:T(8,128)(2,1)}, u32[]{:S(2)}, u32[]{:S(2)}) collective-permute-start(bf16[1,32,32,128]{3,2,1,0:T(8,128)(2,1)} %get-tuple-element.26), channel_id=1, source_target_pairs={{1,0},{2,1},{3,2},{5,4},{6,5},{7,6},{9,8},{10,9},{11,10},{13,12},{... | collective-permute-start | bytes 786440 | tf_op jit(solution)/shard_map/ppermute | solution.py:32
  201.8 1.2 copy-start.39
  201.8 1.2 copy-start.56
  266.2 3.3 copy-start.1
  271.0 38.4 %collective-permute-start.4 = (bf16[1,64,64,64]{3,2,1,0:T(8,128)(2,1)}, bf16[1,64,64,64]{3,2,1,0:T(8,128)(2,1)S(1)}, u32[]{:S(2)}, u32[]{:S(2)}) collective-permute-start(bf16[1,64,64,64]{3,2,1,0:T(8,128)(2,1)} %get-tuple-element.5), channel_id=1, source_target_pairs={{0,1},{1,2},{2,3},{4,5},{5,6},{6,7},{8,9},{9,10},{10,11},{12,13},{... | collective-permute-start | bytes 1572872 | tf_op jit(solution)/shard_map/ppermute | solution.py:29
  274.7 34.7 %collective-permute-start.5 = (bf16[1,64,64,64]{3,2,1,0:T(8,128)(2,1)}, bf16[1,64,64,64]{3,2,1,0:T(8,128)(2,1)}, u32[]{:S(2)}, u32[]{:S(2)}) collective-permute-start(bf16[1,64,64,64]{3,2,1,0:T(8,128)(2,1)} %get-tuple-element.6), channel_id=1, source_target_pairs={{1,0},{2,1},{3,2},{5,4},{6,5},{7,6},{9,8},{10,9},{11,10},{13,12},{... | collective-permute-start | bytes 1572872 | tf_op jit(solution)/shard_map/ppermute | solution.py:32
  282.4 7.3 %copy-start.17 = (bf16[3,17,1,8,3,256]{5,3,4,1,0,2:T(8,128)(2,1)S(1)}, bf16[3,17,1,8,3,256]{5,3,4,1,0,2:T(8,128)(2,1)}, u32[]{:S(2)}) copy-start(bf16[3,17,1,8,3,256]{5,3,4,1,0,2:T(8,128)(2,1)} %copy-done.15) | copy-start | bytes 1880068
  282.4 9.6 %copy-start.20 = (bf16[3,17,1,8,3,256]{5,3,4,1,0,2:T(8,128)(2,1)S(1)}, bf16[3,17,1,8,3,256]{5,3,4,1,0,2:T(8,128)(2,1)}, u32[]{:S(2)}) copy-start(bf16[3,17,1,8,3,256]{5,3,4,1,0,2:T(8,128)(2,1)} %copy-done.18) | copy-start | bytes 1880068
  289.8 2.4 copy-start.6
  289.8 2.4 copy-start.43
  299.0 10.4 %slice-start = ((s8[8388608]{0:T(1024)(128)(4,1)}), s8[4194304]{0:T(1024)(128)(4,1)S(1)}, s32[]{:S(2)}) async-start(s8[8388608]{0:T(1024)(128)(4,1)} %bitcast.418), calls=%async_computation.4 | async-start | bytes 8388608
  300.3 9.0 %slice-start.1 = ((s8[8388608]{0:T(1024)(128)(4,1)}), s8[4194304]{0:T(1024)(128)(4,1)S(1)}, s32[]{:S(2)}) async-start(s8[8388608]{0:T(1024)(128)(4,1)} %bitcast.418), calls=%async_computation.5 | async-start | bytes 8388608
  302.8 49.0 %collective-permute-start.9 = (bf16[1,32,32,128]{3,2,1,0:T(8,128)(2,1)}, bf16[1,32,32,128]{3,2,1,0:T(8,128)(2,1)}, u32[]{:S(2)}, u32[]{:S(2)}) collective-permute-start(bf16[1,32,32,128]{3,2,1,0:T(8,128)(2,1)} %get-tuple-element.27), channel_id=1, source_target_pairs={{0,1},{1,2},{2,3},{4,5},{5,6},{6,7},{8,9},{9,10},{10,11},{12,13},{... | collective-permute-start | bytes 786440 | tf_op jit(solution)/shard_map/ppermute | solution.py:29
  308.1 46.3 %collective-permute-start.10 = (bf16[1,32,32,128]{3,2,1,0:T(8,128)(2,1)}, bf16[1,32,32,128]{3,2,1,0:T(8,128)(2,1)}, u32[]{:S(2)}, u32[]{:S(2)}) collective-permute-start(bf16[1,32,32,128]{3,2,1,0:T(8,128)(2,1)} %get-tuple-element.28), channel_id=1, source_target_pairs={{1,0},{2,1},{3,2},{5,4},{6,5},{7,6},{9,8},{10,9},{11,10},{13,12},{... | collective-permute-start | bytes 786440 | tf_op jit(solution)/shard_map/ppermute | solution.py:32
  348.4 6.0 %copy-start.3 = (bf16[10,64,1,8,10,64]{5,3,4,1,0,2:T(8,128)(2,1)}, bf16[10,64,1,8,10,64]{5,3,4,1,0,2:T(8,128)(2,1)S(1)}, u32[]{:S(2)}) copy-start(bf16[10,64,1,8,10,64]{5,3,4,1,0,2:T(8,128)(2,1)S(1)} %copy.185) | copy-start | bytes 19660804
  437.1 3.3 copy-start.2
  440.4 8.5 %copy-start.8 = (bf16[10,64,1,7,3,64]{5,3,4,1,0,2:T(8,128)(2,1)S(1)}, bf16[10,64,1,7,3,64]{5,3,4,1,0,2:T(8,128)(2,1)}, u32[]{:S(2)}) copy-start(bf16[10,64,1,7,3,64]{5,3,4,1,0,2:T(8,128)(2,1)} %slice.432) | copy-start | bytes 5160964
  442.0 25.1 %collective-permute-start.14 = (bf16[1,64,64,64]{3,2,1,0:T(8,128)(2,1)}, bf16[1,64,64,64]{3,2,1,0:T(8,128)(2,1)}, u32[]{:S(2)}, u32[]{:S(2)}) collective-permute-start(bf16[1,64,64,64]{3,2,1,0:T(8,128)(2,1)} %get-tuple-element.7), channel_id=1, source_target_pairs={{0,1},{1,2},{2,3},{4,5},{5,6},{6,7},{8,9},{9,10},{10,11},{12,13},{... | collective-permute-start | bytes 1572872 | tf_op jit(solution)/shard_map/ppermute | solution.py:29
  447.6 24.5 %collective-permute-start.15 = (bf16[1,64,64,64]{3,2,1,0:T(8,128)(2,1)}, bf16[1,64,64,64]{3,2,1,0:T(8,128)(2,1)}, u32[]{:S(2)}, u32[]{:S(2)}) collective-permute-start(bf16[1,64,64,64]{3,2,1,0:T(8,128)(2,1)} %get-tuple-element.8), channel_id=1, source_target_pairs={{1,0},{2,1},{3,2},{5,4},{6,5},{7,6},{9,8},{10,9},{11,10},{13,12},{... | collective-permute-start | bytes 1572872 | tf_op jit(solution)/shard_map/ppermute | solution.py:32
  514.9 4.7 copy-start.4
  (32 other events, 33.7 us)
Sparse Core Ops, SparseCore 0:
  15.8 28.2 all-gather.12
  45.7 27.5 all-gather.8
  74.8 80.2 all-gather.10
  186.8 83.0 all-gather.6
where the time goes:
time: 555 us; the launch traced here: 547 us
  local copies, waits for them, and re-layouts  212 us (38%)
  waiting for transfers between devices  116 us (21%)
  matrix products  102 us (18%)
  other arithmetic  66.5 us (12%)
  starting transfers between devices  34 us (6%)
  between operations  16.3 us (3%)
    all_gather x1, waiting for transfers between devices, local(): lax.all_gather(first_shard, 'depth', axis=0, tiled=True)  79.6 us
    conv_general_dilated x32, matrix products, transposed(): lax.conv_general_dilated(window[None], kernel_taps, (1, 1, 1), 'VALID', d...  72 us
    unnamed x138, local copies, waits for them, and re-layouts  54.6 us
    conv_general_dilated x2, matrix products, strided(): lax.conv_general_dilated(volume[None], kernel, (2, 2, 2), ((0, 0), (1, 1)...  30.4 us
    convert_element_type x2, local copies, waits for them, and re-layouts, every_layer(): density = jnp.tanh(transposed(hidden, second_kernel)).astype(jnp.bfloat16)  29.5 us
    conv_general_dilated x112, local copies, waits for them, and re-layouts, transposed(): lax.conv_general_dilated(window[None], kernel_taps, (1, 1, 1), 'VALID', d...  27 us
    conv_general_dilated x4, local copies, waits for them, and re-layouts, strided(): lax.conv_general_dilated(volume[None], kernel, (2, 2, 2), ((0, 0), (1, 1)...  25.2 us
    ppermute x5, starting transfers between devices, extended(): lax.ppermute(lax.slice_in_dim(block, block.shape[dim] - width, None, axis...  19.3 us
  transfers between devices with their start and end apart: 20, of which 11 were waited for; matrix products, arithmetic and copies ran while one was open for 39% of the time, Pallas kernels for 0%

commit v1 on v0

v1 whole, which is shorter than its diff:
```python
import functools

import jax
import jax.numpy as jnp
from jax import lax
from jax.experimental import pallas as pl
from jax.experimental.pallas import tpu as pltpu
from jax.sharding import PartitionSpec as P

leak_slope = 0.2
phases = [(pd, ph) for pd in (0, 1) for ph in (0, 1)]
taps = [(td, th) for td in (0, 1) for th in (0, 1)]
budget = 56 * 2**20


def exchanged(value, offset, order):
    count = lax.axis_size("trainer")
    for bit in order:
        pairs = [(source, source ^ (1 << bit)) for source in range(count)]
        moved = lax.ppermute(value, "trainer", pairs)
        chosen = jnp.bitwise_and(jnp.right_shift(offset, bit), 1) == 1
        value = jnp.where(chosen, moved, value)
    return value


def with_halo(block, dim):
    count = lax.axis_size("depth")
    forward = [(i, i + 1) for i in range(count - 1)]
    backward = [(i + 1, i) for i in range(count - 1)]
    size = block.shape[dim]
    low = lax.ppermute(lax.slice_in_dim(block, size - 1, size, axis=dim), "depth", forward)
    high = lax.ppermute(lax.slice_in_dim(block, 0, 1, axis=dim), "depth", backward)
    return jnp.concatenate([low, block, high], axis=dim)


def zeros_like_part(part):
    return jnp.zeros(part.shape, part.dtype)


def first_layer(pd, flags_ref, lat_ref, w_ref, out_ref, wide_ref, *, ph):
    jobs, planes, rows, cells, lanes = out_ref.shape
    c0 = w_ref.shape[0]
    c1 = lanes // 4
    for t in range(4):
        k = [w_ref[:, (4 * t + j) * c1 : (4 * t + j + 1) * c1] for j in range(4)]
        none = zeros_like_part(k[0])
        base = 3 * c0 * t
        wide_ref[base : base + c0, :] = jnp.concatenate([k[3], none], axis=1)
        wide_ref[base + c0 : base + 2 * c0, :] = jnp.concatenate([k[1], k[2]], axis=1)
        wide_ref[base + 2 * c0 : base + 3 * c0, :] = jnp.concatenate([none, k[0]], axis=1)
    edge = 0 if pd == 1 else planes - 1
    inside = flags_ref[0] if pd == 1 else flags_ref[1]

    def plane(n, carry):
        parts = [
            lat_ref[:, n + td, th + ph : th + ph + rows].reshape(jobs * rows * cells, 3 * c0)
            for td, th in taps
        ]
        total = jnp.dot(
            jnp.concatenate(parts, axis=1), wide_ref[...], preferred_element_type=jnp.float32
        )
        keep = jnp.logical_or(n != edge, inside == 1)
        total = jnp.where(keep, jnp.maximum(total, 0.0), 0.0)
        total = total.reshape(jobs * rows, cells, 2 * c1)
        even, odd = total[:, :, :c1], total[:, :, c1:]
        place = lax.broadcasted_iota(jnp.int32, even.shape, 1)
        before = jnp.where(place == 0, 0.0, pltpu.roll(odd, 1, 1))
        after = jnp.where(place == cells - 1, 0.0, pltpu.roll(even, cells - 1, 1))
        packed = jnp.concatenate([before, even, odd, after], axis=2).astype(jnp.bfloat16)
        out_ref[:, n] = packed.reshape(jobs, rows, cells, lanes)
        return carry

    lax.fori_loop(0, planes, plane, 0)


def hidden_part(pd, ph, flags, windows, weight):
    jobs, planes, rows, cells, lanes = windows.shape
    c1 = weight.shape[1] // 16
    out_shape = (jobs, planes - 1, rows - 2, cells, 4 * c1)
    flops = 2 * jobs * (planes - 1) * (rows - 2) * cells * 4 * lanes * 2 * c1
    return pl.pallas_call(
        functools.partial(first_layer, pd, ph=ph),
        out_shape=jax.ShapeDtypeStruct(out_shape, jnp.bfloat16),
        in_specs=[
            pl.BlockSpec(memory_space=pltpu.SMEM),
            pl.BlockSpec(memory_space=pltpu.VMEM),
            pl.BlockSpec(memory_space=pltpu.VMEM),
        ],
        out_specs=pl.BlockSpec(memory_space=pltpu.VMEM),
        scratch_shapes=[pltpu.VMEM((4 * lanes, 2 * c1), jnp.bfloat16)],
        compiler_params=pltpu.CompilerParams(vmem_limit_bytes=budget),
        cost_estimate=pl.CostEstimate(
            flops=flops, bytes_accessed=2 * (windows.size + weight.size), transcendentals=0
        ),
        name=f"hidden_{pd}{ph}",
    )(flags, windows, weight)


def rest(low_end, high_end, flags_ref, p00, p01, p10, p11, w_ref, critic_ref, out_ref,
         hid, wide2, img, wide3, stage):
    part_refs = {(0, 0): p00, (0, 1): p01, (1, 0): p10, (1, 1): p11}
    planes2, rows2, cells, lanes = hid.shape
    rows2 = rows2 - 2
    c1 = lanes // 4
    c2 = c1 // 2
    out_planes = out_ref.shape[0]
    c3 = out_ref.shape[3]

    empty = jnp.zeros((cells, lanes), jnp.bfloat16)
    for q in range(planes2):
        absolute = q + low_end[1]
        pd = 1 - absolute % 2
        n = absolute // 2
        pair = jnp.stack([part_refs[(pd, 0)][0, n], part_refs[(pd, 1)][0, n]], axis=1)
        hid[q, 1 : rows2 + 1] = pair.reshape(rows2, cells, lanes)
        hid[q, 0] = empty
        hid[q, rows2 + 1] = empty

    lane = lax.broadcasted_iota(jnp.int32, (c1, 4 * c2), 1)
    for index, (pd, ph) in enumerate(phases):
        for t, (td, th) in enumerate(taps):
            tap = (3 - pd - 2 * td) * 4 + 3 - ph - 2 * th
            k = w_ref[:, tap * 4 * c2 : (tap + 1) * 4 * c2].astype(jnp.float32)
            down = pltpu.roll(k, 3 * c2, 1)
            up = pltpu.roll(k, c2, 1)
            blocks = [
                jnp.where(lane < c2, up, 0.0),
                jnp.where(lane < 3 * c2, down, 0.0),
                jnp.where(lane >= c2, up, 0.0),
                jnp.where(lane >= 3 * c2, down, 0.0),
            ]
            base = t * 4 * c1
            for j in range(4):
                wide2[index, base + j * c1 : base + (j + 1) * c1, :] = blocks[j].astype(jnp.bfloat16)

    none = jnp.zeros((c2, c3), jnp.bfloat16)
    for t in range(16):
        base = t * 6 * c2
        k = [critic_ref[(4 * t + j) * c2 : (4 * t + j + 1) * c2, :] for j in range(4)]
        left = [k[1], k[2], k[3], none, none, k[0]]
        right = [none, k[0], k[1], k[2], k[3], none]
        for j in range(6):
            wide3[base + j * c2 : base + (j + 1) * c2, :c3] = left[j]
            wide3[base + j * c2 : base + (j + 1) * c2, c3:] = right[j]

    blank = jnp.zeros((cells, 6 * c2), jnp.bfloat16)
    for d in range(img.shape[0]):
        img[d, 0, 0] = blank
        img[d, rows2, 1] = blank

    for index, (pd, ph) in enumerate(phases):
        edge = 0 if pd == 1 else planes2 - 2
        ends = low_end[0] if pd == 1 else high_end
        inside = flags_ref[0] if pd == 1 else flags_ref[1]

        def plane(n, carry, index=index, pd=pd, ph=ph, edge=edge, ends=ends, inside=inside):
            parts = [
                hid[n + td, th + ph : th + ph + rows2].reshape(rows2 * cells, lanes)
                for td, th in taps
            ]
            total = jnp.dot(
                jnp.concatenate(parts, axis=1), wide2[index], preferred_element_type=jnp.float32
            )
            total = jnp.tanh(total)
            if ends:
                total = jnp.where(jnp.logical_or(n != edge, inside == 1), total, 0.0)
            total = total.reshape(rows2, cells, 4 * c2)
            first, second = total[:, :, : 2 * c2], total[:, :, 2 * c2 :]
            place = lax.broadcasted_iota(jnp.int32, first.shape, 1)
            column = lax.broadcasted_iota(jnp.int32, first.shape, 2)
            after = jnp.where(place == cells - 1, 0.0, pltpu.roll(first, cells - 1, 1))
            before = jnp.where(place == 0, 0.0, pltpu.roll(second, 1, 1))
            side = jnp.where(column < c2, after, before)
            packed = jnp.concatenate([first, second, side], axis=2).astype(jnp.bfloat16)
            if ph == 0:
                img[2 * n + 1 - pd, 0:rows2, 1] = packed
            else:
                img[2 * n + 1 - pd, 1 : rows2 + 1, 0] = packed
            return carry

        lax.fori_loop(0, planes2 - 1, plane, 0)

    def judged(m, carry):
        parts = [
            img[2 * m + kd, kh // 2 : kh // 2 + rows2, kh % 2].reshape(rows2 * cells, 6 * c2)
            for kd in range(4)
            for kh in range(4)
        ]
        total = jnp.dot(
            jnp.concatenate(parts, axis=1), wide3[...], preferred_element_type=jnp.float32
        )
        total = jnp.where(total > 0, total, leak_slope * total)
        count = rows2 * cells
        stage[pl.ds(0, count, stride=2), :] = total[:, :c3]
        stage[pl.ds(1, count, stride=2), :] = total[:, c3:]
        out_ref[m] = stage[...].reshape(rows2, 2 * cells, c3).astype(jnp.bfloat16)
        return carry

    lax.fori_loop(0, out_planes, judged, 0)


def judged_planes(job, start, count, flags, parts, second, critic, name):
    jobs, planes, rows, cells, lanes = parts[0].shape
    total_planes = 2 * (planes - 1)
    rows2 = 2 * rows
    c1 = second.shape[0]
    c2 = second.shape[1] // 64
    c3 = critic.shape[1]
    flops = 2 * rows2 * cells * 4 * c2 * ((count + 1) * 4 * 16 * c1 + count * 96 * c2)
    part_spec = pl.BlockSpec((1, planes, rows, cells, lanes), lambda i: (job, 0, 0, 0, 0))
    whole = lambda shape: pl.BlockSpec(shape, lambda i: (0,) * len(shape))
    out_shape = (count, rows2, 2 * cells, c3)
    return pl.pallas_call(
        functools.partial(rest, (start == 0, start), start + count == total_planes),
        grid=(1,),
        out_shape=jax.ShapeDtypeStruct(out_shape, jnp.bfloat16),
        in_specs=[
            pl.BlockSpec(memory_space=pltpu.SMEM),
            part_spec,
            part_spec,
            part_spec,
            part_spec,
            whole(second.shape),
            whole(critic.shape),
        ],
        out_specs=whole(out_shape),
        scratch_shapes=[
            pltpu.VMEM((count + 2, rows2 + 2, cells, lanes), jnp.bfloat16),
            pltpu.VMEM((4, 4 * lanes, 4 * c2), jnp.bfloat16),
            pltpu.VMEM((2 * count + 2, rows2 + 1, 2, cells, 6 * c2), jnp.bfloat16),
            pltpu.VMEM((96 * c2, 2 * c3), jnp.bfloat16),
            pltpu.VMEM((rows2 * cells * 2, c3), jnp.float32),
        ],
        compiler_params=pltpu.CompilerParams(vmem_limit_bytes=budget),
        cost_estimate=pl.CostEstimate(
            flops=flops, bytes_accessed=8 * parts[0].size, transcendentals=0
        ),
        name=name,
    )(flags, *parts, second, critic)


def windows_of(latents):
    padded = jnp.pad(latents, ((0, 0), (0, 0), (1, 1), (1, 1), (0, 0)))
    cells = latents.shape[3]
    return jnp.concatenate([padded[:, :, :, j : j + cells] for j in range(3)], axis=4)


def local(latent, gen_first, gen_second, critic, partner):
    trainer_index = lax.axis_index("trainer")
    offset = jnp.bitwise_xor(partner[trainer_index], trainer_index)
    rounds = lax.axis_size("trainer").bit_length() - 1
    orders = (
        tuple(range(1, rounds)) + (0,),
        tuple(range(rounds - 1, 0, -1)) + (0,),
    )
    z = lax.axis_index("depth")
    flags = jnp.stack([z > 0, z < lax.axis_size("depth") - 1]).astype(jnp.int32)

    c0, columns = gen_first.shape[1:]
    c1 = columns // 64
    shaped = gen_first[0].reshape(c0, 4, 4, 4 * c1)
    gathered = []
    for pd, ph in phases:
        blocks = [shaped[:, 3 - pd - 2 * td, 3 - ph - 2 * th] for td, th in taps]
        part = jnp.concatenate(blocks, axis=1).astype(jnp.bfloat16)
        gathered.append(lax.all_gather(part, "depth", axis=0, tiled=True))
    second = lax.all_gather(gen_second[0].astype(jnp.bfloat16), "depth", axis=0, tiled=True)

    mate_latent = exchanged(latent[0], offset, orders[0])
    windows = windows_of(with_halo(jnp.stack([latent[0], mate_latent]), 1))
    mate_critic = exchanged(critic[0], offset, orders[1])

    parts = [
        hidden_part(pd, ph, flags, windows, weight) for (pd, ph), weight in zip(phases, gathered)
    ]
    planes = 2 * latent.shape[1]
    half = planes // 2
    sent = judged_planes(1, 0, planes, flags, parts, second, mate_critic, "judged_mate")
    received = [
        exchanged(piece, offset, order)
        for piece, order in zip((sent[:half], sent[half:]), orders)
    ]
    own = [
        judged_planes(0, s, half, flags, parts, second, critic[0], "judged_own")
        for s in (0, half)
    ]
    return jnp.stack([jnp.concatenate(own), jnp.concatenate(received)])[None]


def solution(mesh):
    in_specs = (
        P("trainer", "depth", None, None, None),
        P("trainer", "depth", None),
        P("trainer", "depth", None),
        P("trainer", None, None),
        P(),
    )
    out_specs = P("trainer", None, "depth", None, None, None)
    return jax.shard_map(local, mesh=mesh, in_specs=in_specs, out_specs=out_specs, check_vma=False)
```

time: 555 us -> 248 us (0.45); the launches traced: 547 us -> 248 us
  local copies, waits for them, and re-layouts: 212 us -> 5.96 us
  matrix products: 102 us -> 0 us
  Pallas kernels: 0 us -> 86.7 us
  other arithmetic: 66.5 us -> 14.2 us
  starting transfers between devices: 34 us -> 17.6 us
  waiting for transfers between devices: 116 us -> 109 us
    conv_general_dilated x34 -> x0, matrix products: 102 us -> none  [the longest x32 72 us: transposed(): lax.conv_general_dilated(window[None], kernel_taps, (1, 1, 1), 'VALID', d...]
    pallas_call x0 -> x7, Pallas kernels: none -> 86.7 us  [the longest x3 60.3 us: judged_planes(): pl.pallas_call(functools.partial(rest, (start == 0, start), start + count...]
    unnamed x138 -> x12, local copies, waits for them, and re-layouts: 54.6 us -> 0.03 us
    conv_general_dilated x116 -> x0, local copies, waits for them, and re-layouts: 52.1 us -> none  [the longest x112 27 us: transposed(): lax.conv_general_dilated(window[None], kernel_taps, (1, 1, 1), 'VALID', d...]
    convert_element_type x8 -> x0, local copies, waits for them, and re-layouts: 33.7 us -> none  [the longest x2 29.5 us: every_layer(): density = jnp.tanh(transposed(hidden, second_kernel)).astype(jnp.bfloat16)]
    broadcast_in_dim x30 -> x0, local copies, waits for them, and re-layouts: 33.5 us -> none  [the longest x27 16.8 us: transposed(): window[None]]
    all_gather x4 -> x5, waiting for transfers between devices: 83.3 us -> 51.3 us  [the longest x4 30.1 us: local(): gathered.append(lax.all_gather(part, 'depth', axis=0, tiled=True))]
    ppermute x16 -> x14, waiting for transfers between devices: 32.6 us -> 57.7 us  [the longest x12 57.7 us: exchanged(): moved = lax.ppermute(value, 'trainer', pairs)]
  transfers between devices with their start and end apart: 20 -> 19, of which waited for: 11 -> 10; matrix products, arithmetic and copies ran while one was open for 39% -> 5% of each run, Pallas kernels for 0% -> 24%
where the time goes in v1:
time: 248 us
  waiting for transfers between devices  109 us (44%)
  Pallas kernels  86.7 us (35%)
  starting transfers between devices  17.6 us (7%)
  other arithmetic  14.2 us (6%)
  between operations  14 us (6%)
  local copies, waits for them, and re-layouts  5.96 us (2%)
    pallas_call x3, Pallas kernels, judged_planes(): pl.pallas_call(functools.partial(rest, (start == 0, start), start + count...  60.3 us
    ppermute x12, waiting for transfers between devices, exchanged(): moved = lax.ppermute(value, 'trainer', pairs)  57.7 us
    all_gather x4, waiting for transfers between devices, local(): gathered.append(lax.all_gather(part, 'depth', axis=0, tiled=True))  30.1 us
    pallas_call x4, Pallas kernels, hidden_part(): pl.pallas_call(functools.partial(first_layer, pd, ph=ph), out_shape=jax.S...  26.4 us
    all_gather x1, waiting for transfers between devices, local(): lax.all_gather(gen_second[0].astype(jnp.bfloat16), 'depth', axis=0, tiled...  21.2 us
    ppermute x12, starting transfers between devices, exchanged(): moved = lax.ppermute(value, 'trainer', pairs)  12.4 us
  transfers between devices with their start and end apart: 19, of which 10 were waited for; matrix products, arithmetic and copies ran while one was open for 5% of the time, Pallas kernels for 24%

profile of v1, /device:TPU:0, one launch (start us, length us, event | category | flops | bytes accessed | tf_op | source)
XLA Modules:
  0.0 247.6 jit_solution(9466343815825990113)
XLA Ops:
  6.5 1.7 convert.51
  8.2 0.8 reshape.1
  9.0 2.2 fusion.11
  11.3 0.7 pad_maximum_fusion.5
  12.2 0.7 pad_maximum_fusion.4
  13.0 0.7 pad_maximum_fusion.3
  13.9 0.7 pad_maximum_fusion.2
  14.7 3.0 %collective-permute-start = (bf16[2,16,16,256]{3,2,1,0:T(8,128)(2,1)S(1)}, bf16[2,16,16,256]{3,2,1,0:T(8,128)(2,1)S(1)}, u32[]{:S(2)}, u32[]{:S(2)}) collective-permute-start(bf16[2,16,16,256]{3,2,1,0:T(8,128)(2,1)S(1)} %bitcast.48), channel_id=1, source_target_pairs={{0,8},{4,12},{8,0},{12,4},{16,24},{20,28},{24,16},{28,20},{1,9},{5... | collective-permute-start | bytes 786440 | tf_op jit(solution)/shard_map/ppermute | solution.py:20
  17.7 0.6 dynamic_slice.3
  18.9 5.2 %collective-permute-done = bf16[2,16,16,256]{3,2,1,0:T(8,128)(2,1)S(1)} collective-permute-done((bf16[2,16,16,256]{3,2,1,0:T(8,128)(2,1)S(1)}, bf16[2,16,16,256]{3,2,1,0:T(8,128)(2,1)S(1)}, u32[]{:S(2)}, u32[]{:S(2)}) %collective-permute-start) | collective-permute-done | bytes 262176 | tf_op jit(solution)/shard_map/ppermute | solution.py:20
  24.1 1.8 collective-permute-start.1
  25.9 0.3 collective-permute-start.5
  26.2 7.3 %collective-permute-done.1 = bf16[2,16,16,256]{3,2,1,0:T(8,128)(2,1)} collective-permute-done((bf16[2,16,16,256]{3,2,1,0:T(8,128)(2,1)S(1)}, bf16[2,16,16,256]{3,2,1,0:T(8,128)(2,1)}, u32[]{:S(2)}, u32[]{:S(2)}) %collective-permute-start.1) | collective-permute-done | bytes 262176 | tf_op jit(solution)/shard_map/ppermute | solution.py:20
  33.6 0.7 convert_element_type.16
  34.4 0.9 collective-permute-done.2
  35.3 1.0 select_bitcast_fusion
  36.3 3.7 %collective-permute-start.3 = (bf16[2,1,16,16,256]{4,3,2,1,0:T(8,128)(2,1)S(1)}, bf16[2,1,16,16,256]{4,3,2,1,0:T(8,128)(2,1)S(1)}, u32[]{:S(2)}, u32[]{:S(2)}) collective-permute-start(bf16[2,1,16,16,256]{4,3,2,1,0:T(8,128)(2,1)S(1)} %get-tuple-element.28), channel_id=1, source_target_pairs={{0,1},{1,2},{2,3},{4,5},{5,6},{6,7},{8,9},{9,10},{10,11},{12,13},{... | collective-permute-start | bytes 786440 | tf_op jit(solution)/shard_map/ppermute | solution.py:31
  40.1 1.3 collective-permute-start.4
  41.4 12.8 %collective-permute-done.5 = bf16[4096,128]{1,0:T(8,128)(2,1)S(1)} collective-permute-done((bf16[4096,128]{1,0:T(8,128)(2,1)S(1)}, bf16[4096,128]{1,0:T(8,128)(2,1)S(1)}, u32[]{:S(2)}, u32[]{:S(2)}) %collective-permute-start.5) | collective-permute-done | bytes 1048608 | tf_op jit(solution)/shard_map/ppermute | solution.py:20
  54.1 0.1 broadcast_select_fusion
  54.2 1.5 collective-permute-start.6
  55.7 0.6 add_convert_fusion.flags_ref
  56.3 0.8 select_maximum_fusion
  57.1 0.8 fusion.9
  58.0 19.7 %collective-permute-done.6 = bf16[4096,128]{1,0:T(8,128)(2,1)S(1)} collective-permute-done((bf16[4096,128]{1,0:T(8,128)(2,1)S(1)}, bf16[4096,128]{1,0:T(8,128)(2,1)S(1)}, u32[]{:S(2)}, u32[]{:S(2)}) %collective-permute-start.6) | collective-permute-done | bytes 1048608 | tf_op jit(solution)/shard_map/ppermute | solution.py:20
  77.9 1.9 pad_maximum_fusion.lat_ref
  79.8 6.7 %hidden_11.1.p11 = bf16[2,3,16,16,512]{4,3,2,1,0:T(8,128)(2,1)} custom-call(s32[2]{0:T(128)} %add_convert_fusion.flags_ref, bf16[2,4,18,16,768]{4,3,2,1,0:T(8,128)(2,1)} %pad_maximum_fusion.lat_ref, bf16[256,2048]{1,0:T(8,128)(2,1)} %all-gather.13.cloned.1.call-done.w_ref), custom_call_target="tpu_custom_call" | custom-call | flops 2415919104 | bytes 4587520 | tf_op jit(solution)/shard_map/hidden_11/pallas_call | solution.py:81
  86.5 6.6 %hidden_10.1.p10 = bf16[2,3,16,16,512]{4,3,2,1,0:T(8,128)(2,1)} custom-call(s32[2]{0:T(128)} %add_convert_fusion.flags_ref, bf16[2,4,18,16,768]{4,3,2,1,0:T(8,128)(2,1)} %pad_maximum_fusion.lat_ref, bf16[256,2048]{1,0:T(8,128)(2,1)} %all-gather.11.cloned.1.call-done.w_ref), custom_call_target="tpu_custom_call" | custom-call | flops 2415919104 | bytes 4587520 | tf_op jit(solution)/shard_map/hidden_10/pallas_call | solution.py:81
  93.1 7.8 %all-gather.9.cloned.1.call-done.w_ref = bf16[256,2048]{1,0:T(8,128)(2,1)} async-done(((bf16[64,2048]{1,0:T(8,128)(2,1)}), bf16[256,2048]{1,0:T(8,128)(2,1)}) %all-gather.9.cloned.1.call-update) | async-done | bytes 1048592 | tf_op jit(solution)/shard_map/all_gather | solution.py:266
  100.9 6.6 %hidden_01.1.p01 = bf16[2,3,16,16,512]{4,3,2,1,0:T(8,128)(2,1)} custom-call(s32[2]{0:T(128)} %add_convert_fusion.flags_ref, bf16[2,4,18,16,768]{4,3,2,1,0:T(8,128)(2,1)} %pad_maximum_fusion.lat_ref, bf16[256,2048]{1,0:T(8,128)(2,1)} %all-gather.9.cloned.1.call-done.w_ref), custom_call_target="tpu_custom_call" | custom-call | flops 2415919104 | bytes 4587520 | tf_op jit(solution)/shard_map/hidden_01/pallas_call | solution.py:81
  107.5 22.3 %all-gather.7.cloned.1.call-done.w_ref = bf16[256,2048]{1,0:T(8,128)(2,1)} async-done(((bf16[64,2048]{1,0:T(8,128)(2,1)}), bf16[256,2048]{1,0:T(8,128)(2,1)}) %all-gather.7.cloned.1.call-update) | async-done | bytes 1048592 | tf_op jit(solution)/shard_map/all_gather | solution.py:266
  129.8 6.5 %hidden_00.1.p00 = bf16[2,3,16,16,512]{4,3,2,1,0:T(8,128)(2,1)} custom-call(s32[2]{0:T(128)} %add_convert_fusion.flags_ref, bf16[2,4,18,16,768]{4,3,2,1,0:T(8,128)(2,1)} %pad_maximum_fusion.lat_ref, bf16[256,2048]{1,0:T(8,128)(2,1)} %all-gather.7.cloned.1.call-done.w_ref), custom_call_target="tpu_custom_call" | custom-call | flops 2415919104 | bytes 4587520 | tf_op jit(solution)/shard_map/hidden_00/pallas_call | solution.py:81
  136.3 1.1 broadcast_select_fusion.2.critic_ref
  137.4 21.2 %all-gather.15.cloned.1.call-done = bf16[1,128,4096]{2,1,0:T(8,128)(2,1)} async-done(((bf16[1,32,4096]{2,1,0:T(8,128)(2,1)}), bf16[1,128,4096]{2,1,0:T(8,128)(2,1)}) %all-gather.15.cloned.1.call-update) | async-done | bytes 1048592 | tf_op jit(solution)/shard_map/all_gather | solution.py:267
  158.7 26.5 %judged_mate.1 = bf16[4,32,32,128]{3,2,1,0:T(8,128)(2,1)} custom-call(s32[2]{0:T(128)} %add_convert_fusion.flags_ref, bf16[2,3,16,16,512]{4,3,2,1,0:T(8,128)(2,1)} %hidden_00.1.p00, bf16[2,3,16,16,512]{4,3,2,1,0:T(8,128)(2,1)} %hidden_01.1.p01, bf16[2,3,16,16,512]{4,3,2,1,0:T(8,128)(2,1)} %hidden_10.1.p10, bf16[2,3,16,16,512]{4,3,2,1,0:T(8,128)(2,1)} %hidden_11.1.p11, ...), custom_call_target="tpu_custom_call" | custom-call | flops 17179869184 | bytes 6291456 | tf_op jit(solution)/shard_map/judged_mate/pallas_call | solution.py:213
  185.2 1.4 fusion.10
  186.6 1.5 collective-permute-start.11
  188.1 1.5 collective-permute-start.8
  189.6 10.6 %collective-permute-done.11 = bf16[2,32,32,128]{3,2,1,0:T(8,128)(2,1)S(1)} collective-permute-done((bf16[2,32,32,128]{3,2,1,0:T(8,128)(2,1)S(1)}, bf16[2,32,32,128]{3,2,1,0:T(8,128)(2,1)S(1)}, u32[]{:S(2)}, u32[]{:S(2)}) %collective-permute-start.11) | collective-permute-done | bytes 524320 | tf_op jit(solution)/shard_map/ppermute | solution.py:20
  200.2 1.2 collective-permute-done.8
  201.4 0.2 broadcast_select_fusion.4
  201.5 0.6 collective-permute-start.9
  202.1 1.5 collective-permute-start.12
  203.6 17.0 %judged_own.2 = bf16[2,32,32,128]{3,2,1,0:T(8,128)(2,1)} custom-call(s32[2]{0:T(128)} %add_convert_fusion.flags_ref, bf16[2,3,16,16,512]{4,3,2,1,0:T(8,128)(2,1)} %hidden_00.1.p00, bf16[2,3,16,16,512]{4,3,2,1,0:T(8,128)(2,1)} %hidden_01.1.p01, bf16[2,3,16,16,512]{4,3,2,1,0:T(8,128)(2,1)} %hidden_10.1.p10, bf16[2,3,16,16,512]{4,3,2,1,0:T(8,128)(2,1)} %hidden_11.1.p11, ...), custom_call_target="tpu_custom_call" | custom-call | flops 9663676416 | bytes 6291456 | tf_op jit(solution)/shard_map/judged_own/pallas_call | solution.py:213
  220.8 0.5 collective-permute-start.13
  221.4 16.8 %judged_own.3 = bf16[2,32,32,128]{3,2,1,0:T(8,128)(2,1)} custom-call(s32[2]{0:T(128)} %add_convert_fusion.flags_ref, bf16[2,3,16,16,512]{4,3,2,1,0:T(8,128)(2,1)} %hidden_00.1.p00, bf16[2,3,16,16,512]{4,3,2,1,0:T(8,128)(2,1)} %hidden_01.1.p01, bf16[2,3,16,16,512]{4,3,2,1,0:T(8,128)(2,1)} %hidden_10.1.p10, bf16[2,3,16,16,512]{4,3,2,1,0:T(8,128)(2,1)} %hidden_11.1.p11, ...), custom_call_target="tpu_custom_call" | custom-call | flops 9663676416 | bytes 6291456 | tf_op jit(solution)/shard_map/judged_own/pallas_call | solution.py:213
  238.2 1.1 maximum_bitcast_fusion.1
  239.6 1.5 maximum_bitcast_fusion
  (51 shorter events, 1.2 us)
Async XLA Ops:
  6.5 73.3 %all-gather.13.cloned.1.call-start = ((), (), s32[]{:S(2)}) async-start(), calls=%async_computation.3 | async-start | bytes 1310720 | tf_op jit(solution)/shard_map/all_gather | solution.py:266
  12.1 74.4 %all-gather.11.cloned.1.call-start = ((), (), s32[]{:S(2)}) async-start(), calls=%async_computation.2 | async-start | bytes 1310720 | tf_op jit(solution)/shard_map/all_gather | solution.py:266
  12.9 1.8 copy-start.1
  12.9 4.8 %copy-start.5 = (s32[8]{0:T(128)S(1)}, s32[8]{0:T(128)}, u32[]{:S(2)}) copy-start(s32[8]{0:T(128)} %param.9) | copy-start | bytes 100
  12.9 88.0 %all-gather.9.cloned.1.call-start = ((), (), s32[]{:S(2)}) async-start(), calls=%async_computation.1 | async-start | bytes 1310720 | tf_op jit(solution)/shard_map/all_gather | solution.py:266
  13.0 12.9 %copy-start.2 = (bf16[1,4096,128]{2,1,0:T(8,128)(2,1)S(1)}, bf16[1,4096,128]{2,1,0:T(8,128)(2,1)}, u32[]{:S(2)}) copy-start(bf16[1,4096,128]{2,1,0:T(8,128)(2,1)} %param.8) | copy-start | bytes 3145732
  13.8 19.8 %copy-start.3 = (f32[1,32,4096]{2,1,0:T(8,128)S(1)}, f32[1,32,4096]{2,1,0:T(8,128)}, u32[]{:S(2)}) copy-start(f32[1,32,4096]{2,1,0:T(8,128)} %param.7) | copy-start | bytes 1572868
  13.8 116.0 %all-gather.7.cloned.1.call-start = ((), (), s32[]{:S(2)}) async-start(), calls=%async_computation | async-start | bytes 1310720 | tf_op jit(solution)/shard_map/all_gather | solution.py:266
  14.7 144.0 %all-gather.15.cloned.1.call-start = ((), (), s32[]{:S(2)}) async-start(), calls=%async_computation.4 | async-start | bytes 1310720 | tf_op jit(solution)/shard_map/all_gather | solution.py:267
  14.7 9.3 %collective-permute-start = (bf16[2,16,16,256]{3,2,1,0:T(8,128)(2,1)S(1)}, bf16[2,16,16,256]{3,2,1,0:T(8,128)(2,1)S(1)}, u32[]{:S(2)}, u32[]{:S(2)}) collective-permute-start(bf16[2,16,16,256]{3,2,1,0:T(8,128)(2,1)S(1)} %bitcast.48), channel_id=1, source_target_pairs={{0,8},{4,12},{8,0},{12,4},{16,24},{20,28},{24,16},{28,20},{1,9},{5... | collective-permute-start | bytes 786440 | tf_op jit(solution)/shard_map/ppermute | solution.py:20
  24.1 9.4 %collective-permute-start.1 = (bf16[2,16,16,256]{3,2,1,0:T(8,128)(2,1)S(1)}, bf16[2,16,16,256]{3,2,1,0:T(8,128)(2,1)}, u32[]{:S(2)}, u32[]{:S(2)}) collective-permute-start(bf16[2,16,16,256]{3,2,1,0:T(8,128)(2,1)S(1)} %broadcast_select_fusion.9), channel_id=1, source_target_pairs={{0,16},{4,20},{8,24},{12,28},{16,0},{20,4},{24,8},{28,12},{1,17},{... | collective-permute-start | bytes 786440 | tf_op jit(solution)/shard_map/ppermute | solution.py:20
  25.9 28.2 %collective-permute-start.5 = (bf16[4096,128]{1,0:T(8,128)(2,1)S(1)}, bf16[4096,128]{1,0:T(8,128)(2,1)S(1)}, u32[]{:S(2)}, u32[]{:S(2)}) collective-permute-start(bf16[4096,128]{1,0:T(8,128)(2,1)S(1)} %bitcast.51), channel_id=1, source_target_pairs={{0,16},{4,20},{8,24},{12,28},{16,0},{20,4},{24,8},{28,12},{1,17},{... | collective-permute-start | bytes 3145736 | tf_op jit(solution)/shard_map/ppermute | solution.py:20
  33.5 1.7 collective-permute-start.2
  36.3 20.0 %collective-permute-start.3 = (bf16[2,1,16,16,256]{4,3,2,1,0:T(8,128)(2,1)S(1)}, bf16[2,1,16,16,256]{4,3,2,1,0:T(8,128)(2,1)S(1)}, u32[]{:S(2)}, u32[]{:S(2)}) collective-permute-start(bf16[2,1,16,16,256]{4,3,2,1,0:T(8,128)(2,1)S(1)} %get-tuple-element.28), channel_id=1, source_target_pairs={{0,1},{1,2},{2,3},{4,5},{5,6},{6,7},{8,9},{9,10},{10,11},{12,13},{... | collective-permute-start | bytes 786440 | tf_op jit(solution)/shard_map/ppermute | solution.py:31
  40.1 16.3 %collective-permute-start.4 = (bf16[2,1,16,16,256]{4,3,2,1,0:T(8,128)(2,1)S(1)}, bf16[2,1,16,16,256]{4,3,2,1,0:T(8,128)(2,1)S(1)}, u32[]{:S(2)}, u32[]{:S(2)}) collective-permute-start(bf16[2,1,16,16,256]{4,3,2,1,0:T(8,128)(2,1)S(1)} %get-tuple-element.29), channel_id=1, source_target_pairs={{1,0},{2,1},{3,2},{5,4},{6,5},{7,6},{9,8},{10,9},{11,10},{13,12},{... | collective-permute-start | bytes 786440 | tf_op jit(solution)/shard_map/ppermute | solution.py:32
  54.2 23.5 %collective-permute-start.6 = (bf16[4096,128]{1,0:T(8,128)(2,1)S(1)}, bf16[4096,128]{1,0:T(8,128)(2,1)S(1)}, u32[]{:S(2)}, u32[]{:S(2)}) collective-permute-start(bf16[4096,128]{1,0:T(8,128)(2,1)S(1)} %broadcast_select_fusion), channel_id=1, source_target_pairs={{0,8},{4,12},{8,0},{12,4},{16,24},{20,28},{24,16},{28,20},{1,9},{5... | collective-permute-start | bytes 3145736 | tf_op jit(solution)/shard_map/ppermute | solution.py:20
  77.8 58.5 %collective-permute-start.7 = (bf16[4096,128]{1,0:T(8,128)(2,1)S(1)}, bf16[4096,128]{1,0:T(8,128)(2,1)S(1)}, u32[]{:S(2)}, u32[]{:S(2)}) collective-permute-start(bf16[4096,128]{1,0:T(8,128)(2,1)S(1)} %broadcast_select_fusion.1), channel_id=1, source_target_pairs={{0,4},{4,0},{8,12},{12,8},{16,20},{20,16},{24,28},{28,24},{1,5},{5... | collective-permute-start | bytes 3145736 | tf_op jit(solution)/shard_map/ppermute | solution.py:20
  185.2 16.2 %copy-start = (bf16[4,32,32,128]{3,2,1,0:T(8,128)(2,1)S(1)}, bf16[4,32,32,128]{3,2,1,0:T(8,128)(2,1)}, u32[]{:S(2)}) copy-start(bf16[4,32,32,128]{3,2,1,0:T(8,128)(2,1)} %judged_mate.1) | copy-start | bytes 3145732
  186.6 13.6 %collective-permute-start.11 = (bf16[2,32,32,128]{3,2,1,0:T(8,128)(2,1)S(1)}, bf16[2,32,32,128]{3,2,1,0:T(8,128)(2,1)S(1)}, u32[]{:S(2)}, u32[]{:S(2)}) collective-permute-start(bf16[2,32,32,128]{3,2,1,0:T(8,128)(2,1)S(1)} %get-tuple-element.11), channel_id=1, source_target_pairs={{0,16},{4,20},{8,24},{12,28},{16,0},{20,4},{24,8},{28,12},{1,17},{... | collective-permute-start | bytes 1572872 | tf_op jit(solution)/shard_map/ppermute | solution.py:20
  188.1 13.2 %collective-permute-start.8 = (bf16[2,32,32,128]{3,2,1,0:T(8,128)(2,1)S(1)}, bf16[2,32,32,128]{3,2,1,0:T(8,128)(2,1)S(1)}, u32[]{:S(2)}, u32[]{:S(2)}) collective-permute-start(bf16[2,32,32,128]{3,2,1,0:T(8,128)(2,1)S(1)} %get-tuple-element.10), channel_id=1, source_target_pairs={{0,8},{4,12},{8,0},{12,4},{16,24},{20,28},{24,16},{28,20},{1,9},{5... | collective-permute-start | bytes 1572872 | tf_op jit(solution)/shard_map/ppermute | solution.py:20
  201.5 19.1 %collective-permute-start.9 = (bf16[2,32,32,128]{3,2,1,0:T(8,128)(2,1)S(1)}, bf16[2,32,32,128]{3,2,1,0:T(8,128)(2,1)S(1)}, u32[]{:S(2)}, u32[]{:S(2)}) collective-permute-start(bf16[2,32,32,128]{3,2,1,0:T(8,128)(2,1)S(1)} %get-tuple-element.8), channel_id=1, source_target_pairs={{0,16},{4,20},{8,24},{12,28},{16,0},{20,4},{24,8},{28,12},{1,17},{... | collective-permute-start | bytes 1572872 | tf_op jit(solution)/shard_map/ppermute | solution.py:20
  202.1 18.6 %collective-permute-start.12 = (bf16[2,32,32,128]{3,2,1,0:T(8,128)(2,1)S(1)}, bf16[2,32,32,128]{3,2,1,0:T(8,128)(2,1)S(1)}, u32[]{:S(2)}, u32[]{:S(2)}) collective-permute-start(bf16[2,32,32,128]{3,2,1,0:T(8,128)(2,1)S(1)} %get-tuple-element.9), channel_id=1, source_target_pairs={{0,8},{4,12},{8,0},{12,4},{16,24},{20,28},{24,16},{28,20},{1,9},{5... | collective-permute-start | bytes 1572872 | tf_op jit(solution)/shard_map/ppermute | solution.py:20
  220.7 18.6 %collective-permute-start.10 = (bf16[2,32,32,128]{3,2,1,0:T(8,128)(2,1)S(1)}, bf16[2,32,32,128]{3,2,1,0:T(8,128)(2,1)S(1)}, u32[]{:S(2)}, u32[]{:S(2)}) collective-permute-start(bf16[2,32,32,128]{3,2,1,0:T(8,128)(2,1)S(1)} %broadcast_select_fusion.6), channel_id=1, source_target_pairs={{0,4},{4,0},{8,12},{12,8},{16,20},{20,16},{24,28},{28,24},{1,5},{5... | collective-permute-start | bytes 1572872 | tf_op jit(solution)/shard_map/ppermute | solution.py:20
  220.8 17.3 %copy-start.4 = (bf16[2,32,32,128]{3,2,1,0:T(8,128)(2,1)S(1)}, bf16[2,32,32,128]{3,2,1,0:T(8,128)(2,1)}, u32[]{:S(2)}) copy-start(bf16[2,32,32,128]{3,2,1,0:T(8,128)(2,1)} %judged_own.2) | copy-start | bytes 1572868
  220.8 18.5 %collective-permute-start.13 = (bf16[2,32,32,128]{3,2,1,0:T(8,128)(2,1)S(1)}, bf16[2,32,32,128]{3,2,1,0:T(8,128)(2,1)S(1)}, u32[]{:S(2)}, u32[]{:S(2)}) collective-permute-start(bf16[2,32,32,128]{3,2,1,0:T(8,128)(2,1)S(1)} %broadcast_select_fusion.3), channel_id=1, source_target_pairs={{0,4},{4,0},{8,12},{12,8},{16,20},{20,16},{24,28},{28,24},{1,5},{5... | collective-permute-start | bytes 1572872 | tf_op jit(solution)/shard_map/ppermute | solution.py:20
Sparse Core Ops, SparseCore 0:
  12.2 30.6 all-gather.12
  44.4 27.4 all-gather.10
  73.5 27.4 all-gather.8
  102.3 27.4 all-gather.6
  131.2 27.4 all-gather.14

commit v2 on v1

--- a/solution.py
+++ b/solution.py
@@ -11,6 +11,7 @@
 phases = [(pd, ph) for pd in (0, 1) for ph in (0, 1)]
 taps = [(td, th) for td in (0, 1) for th in (0, 1)]
 budget = 56 * 2**20
+mesh_ids = pl.DeviceIdType.MESH
 
 
 def exchanged(value, offset, order):
@@ -23,77 +24,241 @@
     return value
 
 
-def with_halo(block, dim):
+def hidden_kernel(
+    bits, offset_ref, lat_ref, first_ref, second_ref, critic_ref,
+    p00, p01, p10, p11, second_out, critic_out,
+    first_buf, second_buf, lat_all, lat_cur, lat_got, critic_got, packed, wide, acc,
+    first_send, first_recv, second_send, second_recv,
+    lat_send, lat_recv, critic_send, critic_recv, halo_send, halo_recv,
+):
+    part_refs = (p00, p01, p10, p11)
+    jobs, planes, rows, cells, lanes = p00.shape
+    slab = planes - 1
+    c1 = lanes // 4
     count = lax.axis_size("depth")
-    forward = [(i, i + 1) for i in range(count - 1)]
-    backward = [(i + 1, i) for i in range(count - 1)]
-    size = block.shape[dim]
-    low = lax.ppermute(lax.slice_in_dim(block, size - 1, size, axis=dim), "depth", forward)
-    high = lax.ppermute(lax.slice_in_dim(block, 0, 1, axis=dim), "depth", backward)
-    return jnp.concatenate([low, block, high], axis=dim)
-
-
-def zeros_like_part(part):
-    return jnp.zeros(part.shape, part.dtype)
-
-
-def first_layer(pd, flags_ref, lat_ref, w_ref, out_ref, wide_ref, *, ph):
-    jobs, planes, rows, cells, lanes = out_ref.shape
-    c0 = w_ref.shape[0]
-    c1 = lanes // 4
-    for t in range(4):
-        k = [w_ref[:, (4 * t + j) * c1 : (4 * t + j + 1) * c1] for j in range(4)]
-        none = zeros_like_part(k[0])
-        base = 3 * c0 * t
-        wide_ref[base : base + c0, :] = jnp.concatenate([k[3], none], axis=1)
-        wide_ref[base + c0 : base + 2 * c0, :] = jnp.concatenate([k[1], k[2]], axis=1)
-        wide_ref[base + 2 * c0 : base + 3 * c0, :] = jnp.concatenate([none, k[0]], axis=1)
-    edge = 0 if pd == 1 else planes - 1
-    inside = flags_ref[0] if pd == 1 else flags_ref[1]
-
-    def plane(n, carry):
-        parts = [
-            lat_ref[:, n + td, th + ph : th + ph + rows].reshape(jobs * rows * cells, 3 * c0)
-            for td, th in taps
+    z = lax.axis_index("depth")
+    t = lax.axis_index("trainer")
+    right, left = lax.rem(z + 1, count), lax.rem(z + count - 1, count)
+    towards = (right, left)
+    peers = [t + (1 << b) * (1 - 2 * lax.rem(t // (1 << b), 2)) for b in bits]
+    cs = first_ref.shape[0]
+    half = second_ref.shape[1] // 2
+    quarter = first_ref.shape[1] // 4
+
+    barrier = pltpu.get_barrier_semaphore()
+    for there in towards:
+        pl.semaphore_signal(barrier, inc=1, device_id={"depth": there}, device_id_type=mesh_ids)
+    for peer in peers:
+        pl.semaphore_signal(barrier, inc=1, device_id={"trainer": peer}, device_id_type=mesh_ids)
+
+    for pd in (0, 1):
+        for td in (0, 1):
+            kd = 3 - pd - 2 * td
+            piece = first_ref[:, kd * quarter : (kd + 1) * quarter]
+            first_buf[pd, 0, td] = piece.astype(jnp.bfloat16)
+        second_buf[pd, 0] = second_ref[:, pd * half : (pd + 1) * half].astype(jnp.bfloat16)
+    lat_cur[...] = lat_ref[...]
+    critic_out[...] = critic_ref[...]
+    blank = jnp.zeros((cells, lat_ref.shape[3]), jnp.bfloat16)
+    for j in range(jobs):
+        for d in range(slab):
+            lat_all[j, d + 1, 0] = blank
+            lat_all[j, d + 1, rows + 1] = blank
+    for d in range(slab):
+        lat_all[0, d + 1, 1 : rows + 1] = lat_ref[d]
+    pl.semaphore_wait(barrier, 2 + len(bits))
+
+    def sent(src, dst, send, recv, **where):
+        copy = pltpu.make_async_remote_copy(
+            src_ref=src, dst_ref=dst, send_sem=send, recv_sem=recv,
+            device_id=where, device_id_type=mesh_ids,
+        )
+        copy.start()
+        return copy
+
+    def halo(job):
+        return [
+            sent(lat_all.at[job, slab], lat_all.at[job, 0], halo_send.at[job, 0],
+                 halo_recv.at[job, 0], depth=right),
+            sent(lat_all.at[job, 1], lat_all.at[job, slab + 1], halo_send.at[job, 1],
+                 halo_recv.at[job, 1], depth=left),
         ]
-        total = jnp.dot(
-            jnp.concatenate(parts, axis=1), wide_ref[...], preferred_element_type=jnp.float32
-        )
-        keep = jnp.logical_or(n != edge, inside == 1)
-        total = jnp.where(keep, jnp.maximum(total, 0.0), 0.0)
-        total = total.reshape(jobs * rows, cells, 2 * c1)
-        even, odd = total[:, :, :c1], total[:, :, c1:]
-        place = lax.broadcasted_iota(jnp.int32, even.shape, 1)
-        before = jnp.where(place == 0, 0.0, pltpu.roll(odd, 1, 1))
-        after = jnp.where(place == cells - 1, 0.0, pltpu.roll(even, cells - 1, 1))
-        packed = jnp.concatenate([before, even, odd, after], axis=2).astype(jnp.bfloat16)
-        out_ref[:, n] = packed.reshape(jobs, rows, cells, lanes)
+
+    def ring(step):
+        copies = []
+        for pd in (0, 1):
+            for td in (0, 1):
+                copies.append(
+                    sent(first_buf.at[pd, step, td], first_buf.at[pd, step + 1, td],
+                         first_send.at[pd, step, td], first_recv.at[pd, step, td],
+                         depth=towards[pd])
+                )
+        for pd in (0, 1):
+            copies.append(
+                sent(second_buf.at[pd, step], second_buf.at[pd, step + 1],
+                     second_send.at[pd, step], second_recv.at[pd, step], depth=towards[pd])
+            )
+        return copies
+
+    def swap_latent(r):
+        return sent(lat_cur, lat_got.at[r], lat_send.at[r], lat_recv.at[r], trainer=peers[r])
+
+    def swap_critic(r):
+        return sent(critic_out, critic_got.at[r], critic_send.at[r], critic_recv.at[r],
+                    trainer=peers[r])
+
+    def chosen(r):
+        return offset_ref[bits[r]] == 1
+
+    moving = swap_latent(0)
+    halos = halo(0)
+    moves = ring(0)
+    for r in range(len(bits)):
+        moving.wait()
+        lat_cur[...] = jnp.where(chosen(r), lat_got[r], lat_cur[...])
+        if r + 1 < len(bits):
+            moving = swap_latent(r + 1)
+    for d in range(slab):
+        lat_all[1, d + 1, 1 : rows + 1] = lat_cur[d]
+    halos += halo(1)
+    critic_move = swap_critic(0)
+    for copy in halos:
+        copy.wait()
+    for end, inside in ((0, z > 0), (slab + 1, z < count - 1)):
+        lat_all[:, end] = jnp.where(inside, lat_all[:, end], jnp.zeros_like(lat_all[:, end]))
+
+    per = 128 // cs
+    group_rows = jobs * (rows + 1)
+
+    def pack(n, carry):
+        for s in range(count):
+            tile, off = s * cs // 128 * 128, s * cs % 128
+            for g in range(4 // per):
+                center = None
+                for i in range(per):
+                    td, th = divmod(g * per + i, 2)
+                    x = lat_all[:, n + td, th : th + rows + 1, :, tile : tile + 128]
+                    x = x.astype(jnp.float32).reshape(group_rows * cells, 128)
+                    shift = (i * cs - off) % 128
+                    x = pltpu.roll(x, shift, 1) if shift else x
+                    lane = lax.broadcasted_iota(jnp.int32, x.shape, 1)
+                    center = x if center is None else jnp.where(lane < i * cs, center, x)
+                center = center.reshape(group_rows, cells, 128)
+                place = lax.broadcasted_iota(jnp.int32, center.shape, 1)
+                before = jnp.where(place == 0, 0.0, pltpu.roll(center, 1, 1))
+                after = jnp.where(place == cells - 1, 0.0, pltpu.roll(center, cells - 1, 1))
+                for j, value in enumerate((before, center, after)):
+                    base = j * 4 * cs + g * 128
+                    packed[s, :, n, :, :, base : base + 128] = value.astype(jnp.bfloat16).reshape(
+                        jobs, rows + 1, cells, 128
+                    )
         return carry
 
-    lax.fori_loop(0, planes, plane, 0)
-
-
-def hidden_part(pd, ph, flags, windows, weight):
-    jobs, planes, rows, cells, lanes = windows.shape
-    c1 = weight.shape[1] // 16
-    out_shape = (jobs, planes - 1, rows - 2, cells, 4 * c1)
-    flops = 2 * jobs * (planes - 1) * (rows - 2) * cells * 4 * lanes * 2 * c1
+    lax.fori_loop(0, planes, pack, 0)
+
+    none = jnp.zeros((cs, c1), jnp.bfloat16)
+    for step in range(count):
+        if step:
+            for copy in moves:
+                copy.wait()
+            if step < count - 1:
+                moves = ring(step)
+        for pd in (0, 1):
+            owner = lax.rem(z + count - step, count) if pd == 0 else lax.rem(z + step, count)
+            second_out[owner, :, pd * half : (pd + 1) * half] = second_buf[pd, step]
+            for ph in (0, 1):
+                for td, th in taps:
+                    col = (3 - ph - 2 * th) * 4 * c1
+                    k = [
+                        first_buf[pd, step, td, :, col + j * c1 : col + (j + 1) * c1]
+                        for j in range(4)
+                    ]
+                    for j, (a, b) in enumerate(((k[3], none), (k[1], k[2]), (none, k[0]))):
+                        base = (4 * j + 2 * td + th) * cs
+                        wide[base : base + cs, :c1] = a
+                        wide[base : base + cs, c1:] = b
+
+                def plane(n, carry, ph=ph, index=2 * pd + ph, owner=owner, step=step):
+                    lhs = packed[owner, :, n, ph : ph + rows].reshape(
+                        jobs * rows * cells, 12 * cs
+                    )
+                    total = jnp.dot(lhs, wide[...], preferred_element_type=jnp.float32)
+                    acc[index, n] = total if step == 0 else acc[index, n] + total
+                    return carry
+
+                lax.fori_loop(0, planes, plane, 0)
+        if step < len(bits):
+            critic_move.wait()
+            critic_out[...] = jnp.where(chosen(step), critic_got[step], critic_out[...])
+            if step + 1 < len(bits):
+                critic_move = swap_critic(step + 1)
+
+    for index, (pd, ph) in enumerate(phases):
+        edge = 0 if pd == 1 else planes - 1
+        inside = z > 0 if pd == 1 else z < count - 1
+
+        def finish(n, carry, index=index, edge=edge, inside=inside):
+            keep = jnp.logical_or(n != edge, inside)
+            total = jnp.where(keep, jnp.maximum(acc[index, n], 0.0), 0.0)
+            total = total.reshape(jobs * rows, cells, 2 * c1)
+            even, odd = total[:, :, :c1], total[:, :, c1:]
+            place = lax.broadcasted_iota(jnp.int32, even.shape, 1)
+            before = jnp.where(place == 0, 0.0, pltpu.roll(odd, 1, 1))
+            after = jnp.where(place == cells - 1, 0.0, pltpu.roll(even, cells - 1, 1))
+            result = jnp.concatenate([before, even, odd, after], axis=2).astype(jnp.bfloat16)
+            part_refs[index][:, n] = result.reshape(jobs, rows, cells, lanes)
+            return carry
+
+        lax.fori_loop(0, planes, finish, 0)
+
+
+def hidden_parts(offset_bits, latent, first, second, critic, bits):
+    slab, rows, cells, c0 = latent.shape
+    count = lax.axis_size("depth")
+    cs, columns = first.shape
+    c1 = columns // 64
+    rounds = len(bits)
+    part = jax.ShapeDtypeStruct((2, slab + 1, rows, cells, 4 * c1), jnp.bfloat16)
+    in_vmem = pl.BlockSpec(memory_space=pltpu.VMEM)
+    half = second.shape[1] // 2
+    dma = pltpu.SemaphoreType.DMA
+    flops = 2 * 2 * (slab + 1) * rows * cells * 4 * 12 * c0 * 2 * c1
     return pl.pallas_call(
-        functools.partial(first_layer, pd, ph=ph),
-        out_shape=jax.ShapeDtypeStruct(out_shape, jnp.bfloat16),
-        in_specs=[
-            pl.BlockSpec(memory_space=pltpu.SMEM),
-            pl.BlockSpec(memory_space=pltpu.VMEM),
-            pl.BlockSpec(memory_space=pltpu.VMEM),
+        functools.partial(hidden_kernel, bits),
+        out_shape=[part] * 4
+        + [
+            jax.ShapeDtypeStruct((count,) + second.shape, jnp.bfloat16),
+            jax.ShapeDtypeStruct(critic.shape, jnp.bfloat16),
         ],
-        out_specs=pl.BlockSpec(memory_space=pltpu.VMEM),
-        scratch_shapes=[pltpu.VMEM((4 * lanes, 2 * c1), jnp.bfloat16)],
-        compiler_params=pltpu.CompilerParams(vmem_limit_bytes=budget),
-        cost_estimate=pl.CostEstimate(
-            flops=flops, bytes_accessed=2 * (windows.size + weight.size), transcendentals=0
+        in_specs=[pl.BlockSpec(memory_space=pltpu.SMEM)] + [in_vmem] * 4,
+        out_specs=[in_vmem] * 6,
+        scratch_shapes=[
+            pltpu.VMEM((2, count, 2, cs, columns // 4), jnp.bfloat16),
+            pltpu.VMEM((2, count, second.shape[0], half), jnp.bfloat16),
+            pltpu.VMEM((2, slab + 2, rows + 2, cells, c0), jnp.bfloat16),
+            pltpu.VMEM(latent.shape, jnp.bfloat16),
+            pltpu.VMEM((rounds,) + latent.shape, jnp.bfloat16),
+            pltpu.VMEM((rounds,) + critic.shape, jnp.bfloat16),
+            pltpu.VMEM((count, 2, slab + 1, rows + 1, cells, 12 * cs), jnp.bfloat16),
+            pltpu.VMEM((12 * cs, 2 * c1), jnp.bfloat16),
+            pltpu.VMEM((4, slab + 1, 2 * rows * cells, 2 * c1), jnp.float32),
+            dma((2, count - 1, 2)),
+            dma((2, count - 1, 2)),
+            dma((2, count - 1)),
+            dma((2, count - 1)),
+            dma((rounds,)),
+            dma((rounds,)),
+            dma((rounds,)),
+            dma((rounds,)),
+            dma((2, 2)),
+            dma((2, 2)),
+        ],
+        compiler_params=pltpu.CompilerParams(
+            vmem_limit_bytes=budget, collective_id=0, has_side_effects=True
         ),
-        name=f"hidden_{pd}{ph}",
-    )(flags, windows, weight)
+        cost_estimate=pl.CostEstimate(flops=flops, bytes_accessed=2**24, transcendentals=0),
+        name="hidden",
+    )(offset_bits, latent, first, second, critic)
 
 
 def rest(low_end, high_end, flags_ref, p00, p01, p10, p11, w_ref, critic_ref, out_ref,
@@ -239,12 +404,6 @@
     )(flags, *parts, second, critic)
 
 
-def windows_of(latents):
-    padded = jnp.pad(latents, ((0, 0), (0, 0), (1, 1), (1, 1), (0, 0)))
-    cells = latents.shape[3]
-    return jnp.concatenate([padded[:, :, :, j : j + cells] for j in range(3)], axis=4)
-
-
 def local(latent, gen_first, gen_second, critic, partner):
     trainer_index = lax.axis_index("trainer")
     offset = jnp.bitwise_xor(partner[trainer_index], trainer_index)
@@ -256,23 +415,12 @@
     z = lax.axis_index("depth")
     flags = jnp.stack([z > 0, z < lax.axis_size("depth") - 1]).astype(jnp.int32)
 
-    c0, columns = gen_first.shape[1:]
-    c1 = columns // 64
-    shaped = gen_first[0].reshape(c0, 4, 4, 4 * c1)
-    gathered = []
-    for pd, ph in phases:
-        blocks = [shaped[:, 3 - pd - 2 * td, 3 - ph - 2 * th] for td, th in taps]
-        part = jnp.concatenate(blocks, axis=1).astype(jnp.bfloat16)
-        gathered.append(lax.all_gather(part, "depth", axis=0, tiled=True))
-    second = lax.all_gather(gen_second[0].astype(jnp.bfloat16), "depth", axis=0, tiled=True)
-
-    mate_latent = exchanged(latent[0], offset, orders[0])
-    windows = windows_of(with_halo(jnp.stack([latent[0], mate_latent]), 1))
-    mate_critic = exchanged(critic[0], offset, orders[1])
-
-    parts = [
-        hidden_part(pd, ph, flags, windows, weight) for (pd, ph), weight in zip(phases, gathered)
-    ]
+    bits = orders[0]
+    offset_bits = jnp.stack([jnp.bitwise_and(jnp.right_shift(offset, b), 1) for b in range(rounds)])
+    *parts, second, mate_critic = hidden_parts(
+        offset_bits, latent[0], gen_first[0], gen_second[0], critic[0], bits
+    )
+    second = second.reshape(-1, second.shape[2])
     planes = 2 * latent.shape[1]
     half = planes // 2
     sent = judged_planes(1, 0, planes, flags, parts, second, mate_critic, "judged_mate")

time: 248 us -> 208 us (0.84)
  waiting for transfers between devices: 109 us -> 10.2 us
  Pallas kernels: 86.7 us -> 184 us
  between operations: 14 us -> 0.74 us
  starting transfers between devices: 17.6 us -> 5.66 us
  other arithmetic: 14.2 us -> 4.24 us
  local copies, waits for them, and re-layouts: 5.96 us -> 2.67 us
    pallas_call x4 -> x1, Pallas kernels: 26.4 us -> 124 us  [hidden_parts(): pl.pallas_call(functools.partial(hidden_kernel, bits), out_shape=[part] *...]
    all_gather x5 -> x0, waiting for transfers between devices: 51.3 us -> none  [the longest x4 30.1 us: local(): gathered.append(lax.all_gather(part, 'depth', axis=0, tiled=True))]
    ppermute x12 -> x6, waiting for transfers between devices: 57.7 us -> 10.2 us  [exchanged(): moved = lax.ppermute(value, 'trainer', pairs)]
    ppermute x12 -> x6, starting transfers between devices: 12.4 us -> 5.66 us  [exchanged(): moved = lax.ppermute(value, 'trainer', pairs)]
    concatenate x6 -> x0, other arithmetic: 5.67 us -> none  [the longest x4 2.92 us: local(): part = jnp.concatenate(blocks, axis=1).astype(jnp.bfloat16)]
    ppermute x2 -> x0, starting transfers between devices: 5.03 us -> none  [the longest x1 3.74 us: with_halo(): lax.ppermute(lax.slice_in_dim(block, size - 1, size, axis=dim), 'depth',...]
    slice x2 -> x0, local copies, waits for them, and re-layouts: 3.05 us -> none  [the longest x1 2.21 us: local(): blocks = [shaped[:, 3 - pd - 2 * td, 3 - ph - 2 * th] for td, th in taps]]
  transfers between devices with their start and end apart: 19 -> 6, of which waited for: 10 -> 2; matrix products, arithmetic and copies ran while one was open for 5% -> 1% of each run, Pallas kernels for 24% -> 16%
where the time goes in v2:
time: 208 us
  Pallas kernels  184 us (88%)
  waiting for transfers between devices  10.2 us (5%)
  starting transfers between devices  5.66 us (3%)
  other arithmetic  4.24 us (2%)
  local copies, waits for them, and re-layouts  2.67 us (1%)
    pallas_call x1, Pallas kernels, hidden_parts(): pl.pallas_call(functools.partial(hidden_kernel, bits), out_shape=[part] *...  124 us
    pallas_call x3, Pallas kernels, judged_planes(): pl.pallas_call(functools.partial(rest, (start == 0, start), start + count...  60.2 us
    ppermute x6, waiting for transfers between devices, exchanged(): moved = lax.ppermute(value, 'trainer', pairs)  10.2 us
    ppermute x6, starting transfers between devices, exchanged(): moved = lax.ppermute(value, 'trainer', pairs)  5.66 us
  transfers between devices with their start and end apart: 6, of which 2 were waited for; matrix products, arithmetic and copies ran while one was open for 1% of the time, Pallas kernels for 16%

profile of v2, /device:TPU:0, one launch (start us, length us, event | category | flops | bytes accessed | tf_op | source)
XLA Modules:
  0.0 207.8 jit_solution(2453024472952348670)
XLA Ops:
  0.0 1.3 dynamic_slice.3
  1.9 0.6 add_convert_fusion.flags_ref
  2.5 0.6 pad_add_fusion.offset_ref
  3.1 124.1 %hidden.1 = (bf16[2,3,16,16,512]{4,3,2,1,0:T(8,128)(2,1)}, bf16[2,3,16,16,512]{4,3,2,1,0:T(8,128)(2,1)}, bf16[2,3,16,16,512]{4,3,2,1,0:T(8,128)(2,1)}, bf16[2,3,...) custom-call(s32[3]{0:T(128)} %pad_add_fusion.offset_ref, ...), custom_call_target="tpu_custom_call" | custom-call | flops 9663676416 | bytes 16777216 | tf_op jit(solution)/shard_map/hidden/pallas_call | solution.py:226
  127.2 26.7 %judged_mate.1 = bf16[4,32,32,128]{3,2,1,0:T(8,128)(2,1)} custom-call(s32[2]{0:T(128)} %add_convert_fusion.flags_ref, bf16[2,3,16,16,512]{4,3,2,1,0:T(8,128)(2,1)} %get-tuple-element.11.p00, bf16[2,3,16,16,512]{4,3,2,1,0:T(8,128)(2,1)} %get-tuple-element.12.p01, bf16[2,3,16,16,512]{4,3,2,1,0:T(8,128)(2,1)} %get-tuple-element.13.p10, ...), custom_call_target="tpu_custom_call" | custom-call | flops 17179869184 | bytes 6291456 | tf_op jit(solution)/shard_map/judged_mate/pallas_call | solution.py:378
  153.9 0.0 copy-start
  153.9 1.4 fusion
  155.3 1.6 collective-permute-start
  156.8 1.5 collective-permute-start.3
  158.3 6.9 %collective-permute-done = bf16[2,32,32,128]{3,2,1,0:T(8,128)(2,1)S(1)} collective-permute-done((bf16[2,32,32,128]{3,2,1,0:T(8,128)(2,1)S(1)}, bf16[2,32,32,128]{3,2,1,0:T(8,128)(2,1)S(1)}, u32[]{:S(2)}, u32[]{:S(2)}) %collective-permute-start) | collective-permute-done | bytes 524320 | tf_op jit(solution)/shard_map/ppermute | solution.py:21
  165.2 3.3 %collective-permute-done.3 = bf16[2,32,32,128]{3,2,1,0:T(8,128)(2,1)S(1)} collective-permute-done((bf16[2,32,32,128]{3,2,1,0:T(8,128)(2,1)S(1)}, bf16[2,32,32,128]{3,2,1,0:T(8,128)(2,1)S(1)}, u32[]{:S(2)}, u32[]{:S(2)}) %collective-permute-start.3) | collective-permute-done | bytes 524320 | tf_op jit(solution)/shard_map/ppermute | solution.py:21
  168.5 0.0 copy-done
  168.5 0.1 broadcast_select_fusion.1
  168.6 1.8 collective-permute-start.1
  170.4 0.2 collective-permute-start.4
  170.6 16.8 %judged_own.3 = bf16[2,32,32,128]{3,2,1,0:T(8,128)(2,1)} custom-call(s32[2]{0:T(128)} %add_convert_fusion.flags_ref, bf16[2,3,16,16,512]{4,3,2,1,0:T(8,128)(2,1)} %get-tuple-element.11.p00, bf16[2,3,16,16,512]{4,3,2,1,0:T(8,128)(2,1)} %get-tuple-element.12.p01, bf16[2,3,16,16,512]{4,3,2,1,0:T(8,128)(2,1)} %get-tuple-element.13.p10, ...), custom_call_target="tpu_custom_call" | custom-call | flops 9663676416 | bytes 6291456 | tf_op jit(solution)/shard_map/judged_own/pallas_call | solution.py:378
  187.4 0.0 collective-permute-done.1
  187.4 0.1 broadcast_select_fusion.3
  187.4 0.1 collective-permute-start.2
  187.5 0.0 collective-permute-done.4
  187.5 0.1 broadcast_select_fusion
  187.6 0.0 copy-start.1
  187.6 0.5 collective-permute-start.5
  188.1 16.8 %judged_own.2 = bf16[2,32,32,128]{3,2,1,0:T(8,128)(2,1)} custom-call(s32[2]{0:T(128)} %add_convert_fusion.flags_ref, bf16[2,3,16,16,512]{4,3,2,1,0:T(8,128)(2,1)} %get-tuple-element.11.p00, bf16[2,3,16,16,512]{4,3,2,1,0:T(8,128)(2,1)} %get-tuple-element.12.p01, bf16[2,3,16,16,512]{4,3,2,1,0:T(8,128)(2,1)} %get-tuple-element.13.p10, ...), custom_call_target="tpu_custom_call" | custom-call | flops 9663676416 | bytes 6291456 | tf_op jit(solution)/shard_map/judged_own/pallas_call | solution.py:378
  204.9 0.0 copy-done.1
  204.9 1.1 maximum_bitcast_fusion.1
  206.0 0.0 collective-permute-done.2
  206.0 0.1 broadcast_select_fusion.5
  206.1 0.0 collective-permute-done.5
  206.1 0.1 broadcast_select_fusion.4
  206.2 0.1 maximum_bitcast_fusion.2
  206.3 1.5 maximum_bitcast_fusion
Async XLA Ops:
  153.9 14.6 %copy-start = (bf16[4,32,32,128]{3,2,1,0:T(8,128)(2,1)S(1)}, bf16[4,32,32,128]{3,2,1,0:T(8,128)(2,1)}, u32[]{:S(2)}) copy-start(bf16[4,32,32,128]{3,2,1,0:T(8,128)(2,1)} %judged_mate.1) | copy-start | bytes 3145732
  155.3 9.9 %collective-permute-start = (bf16[2,32,32,128]{3,2,1,0:T(8,128)(2,1)S(1)}, bf16[2,32,32,128]{3,2,1,0:T(8,128)(2,1)S(1)}, u32[]{:S(2)}, u32[]{:S(2)}) collective-permute-start(bf16[2,32,32,128]{3,2,1,0:T(8,128)(2,1)S(1)} %get-tuple-element.19), channel_id=1, source_target_pairs={{0,8},{4,12},{8,0},{12,4},{16,24},{20,28},{24,16},{28,20},{1,9},{5... | collective-permute-start | bytes 1572872 | tf_op jit(solution)/shard_map/ppermute | solution.py:21
  156.8 11.7 %collective-permute-start.3 = (bf16[2,32,32,128]{3,2,1,0:T(8,128)(2,1)S(1)}, bf16[2,32,32,128]{3,2,1,0:T(8,128)(2,1)S(1)}, u32[]{:S(2)}, u32[]{:S(2)}) collective-permute-start(bf16[2,32,32,128]{3,2,1,0:T(8,128)(2,1)S(1)} %get-tuple-element.20), channel_id=1, source_target_pairs={{0,16},{4,20},{8,24},{12,28},{16,0},{20,4},{24,8},{28,12},{1,17},{... | collective-permute-start | bytes 1572872 | tf_op jit(solution)/shard_map/ppermute | solution.py:21
  168.6 18.7 %collective-permute-start.1 = (bf16[2,32,32,128]{3,2,1,0:T(8,128)(2,1)S(1)}, bf16[2,32,32,128]{3,2,1,0:T(8,128)(2,1)S(1)}, u32[]{:S(2)}, u32[]{:S(2)}) collective-permute-start(bf16[2,32,32,128]{3,2,1,0:T(8,128)(2,1)S(1)} %get-tuple-element.17), channel_id=1, source_target_pairs={{0,16},{4,20},{8,24},{12,28},{16,0},{20,4},{24,8},{28,12},{1,17},{... | collective-permute-start | bytes 1572872 | tf_op jit(solution)/shard_map/ppermute | solution.py:21
  170.4 17.1 %collective-permute-start.4 = (bf16[2,32,32,128]{3,2,1,0:T(8,128)(2,1)S(1)}, bf16[2,32,32,128]{3,2,1,0:T(8,128)(2,1)S(1)}, u32[]{:S(2)}, u32[]{:S(2)}) collective-permute-start(bf16[2,32,32,128]{3,2,1,0:T(8,128)(2,1)S(1)} %get-tuple-element.18), channel_id=1, source_target_pairs={{0,8},{4,12},{8,0},{12,4},{16,24},{20,28},{24,16},{28,20},{1,9},{5... | collective-permute-start | bytes 1572872 | tf_op jit(solution)/shard_map/ppermute | solution.py:21
  187.4 18.6 %collective-permute-start.2 = (bf16[2,32,32,128]{3,2,1,0:T(8,128)(2,1)S(1)}, bf16[2,32,32,128]{3,2,1,0:T(8,128)(2,1)S(1)}, u32[]{:S(2)}, u32[]{:S(2)}) collective-permute-start(bf16[2,32,32,128]{3,2,1,0:T(8,128)(2,1)S(1)} %broadcast_select_fusion.3), channel_id=1, source_target_pairs={{0,4},{4,0},{8,12},{12,8},{16,20},{20,16},{24,28},{28,24},{1,5},{5... | collective-permute-start | bytes 1572872 | tf_op jit(solution)/shard_map/ppermute | solution.py:21
  187.6 17.3 %copy-start.1 = (bf16[2,32,32,128]{3,2,1,0:T(8,128)(2,1)S(1)}, bf16[2,32,32,128]{3,2,1,0:T(8,128)(2,1)}, u32[]{:S(2)}) copy-start(bf16[2,32,32,128]{3,2,1,0:T(8,128)(2,1)} %judged_own.3) | copy-start | bytes 1572868
  187.6 18.5 %collective-permute-start.5 = (bf16[2,32,32,128]{3,2,1,0:T(8,128)(2,1)S(1)}, bf16[2,32,32,128]{3,2,1,0:T(8,128)(2,1)S(1)}, u32[]{:S(2)}, u32[]{:S(2)}) collective-permute-start(bf16[2,32,32,128]{3,2,1,0:T(8,128)(2,1)S(1)} %broadcast_select_fusion), channel_id=1, source_target_pairs={{0,4},{4,0},{8,12},{12,8},{16,20},{20,16},{24,28},{28,24},{1,5},{5... | collective-permute-start | bytes 1572872 | tf_op jit(solution)/shard_map/ppermute | solution.py:21

commit v3 on v2

--- a/solution.py
+++ b/solution.py
@@ -12,16 +12,6 @@
 taps = [(td, th) for td in (0, 1) for th in (0, 1)]
 budget = 56 * 2**20
 mesh_ids = pl.DeviceIdType.MESH
-
-
-def exchanged(value, offset, order):
-    count = lax.axis_size("trainer")
-    for bit in order:
-        pairs = [(source, source ^ (1 << bit)) for source in range(count)]
-        moved = lax.ppermute(value, "trainer", pairs)
-        chosen = jnp.bitwise_and(jnp.right_shift(offset, bit), 1) == 1
-        value = jnp.where(chosen, moved, value)
-    return value
 
 
 def hidden_kernel(
@@ -261,29 +251,27 @@
     )(offset_bits, latent, first, second, critic)
 
 
-def rest(low_end, high_end, flags_ref, p00, p01, p10, p11, w_ref, critic_ref, out_ref,
-         hid, wide2, img, wide3, stage):
+def judged_kernel(
+    bits, offset_ref, p00, p01, p10, p11, w_ref, mate_critic_ref, critic_ref, out_ref,
+    hid, wide2, img, wide3, stage, got, send_sem, recv_sem,
+):
     part_refs = {(0, 0): p00, (0, 1): p01, (1, 0): p10, (1, 1): p11}
     planes2, rows2, cells, lanes = hid.shape
     rows2 = rows2 - 2
     c1 = lanes // 4
     c2 = c1 // 2
-    out_planes = out_ref.shape[0]
-    c3 = out_ref.shape[3]
-
-    empty = jnp.zeros((cells, lanes), jnp.bfloat16)
-    for q in range(planes2):
-        absolute = q + low_end[1]
-        pd = 1 - absolute % 2
-        n = absolute // 2
-        pair = jnp.stack([part_refs[(pd, 0)][0, n], part_refs[(pd, 1)][0, n]], axis=1)
-        hid[q, 1 : rows2 + 1] = pair.reshape(rows2, cells, lanes)
-        hid[q, 0] = empty
-        hid[q, rows2 + 1] = empty
+    out_planes, c3 = out_ref.shape[1], out_ref.shape[4]
+    z = lax.axis_index("depth")
+    t = lax.axis_index("trainer")
+    rounds = len(bits[0])
+    peers = [t + (1 << b) * (1 - 2 * lax.rem(t // (1 << b), 2)) for b in range(rounds)]
+    barrier = pltpu.get_barrier_semaphore()
+    for peer in peers:
+        pl.semaphore_signal(barrier, inc=1, device_id={"trainer": peer}, device_id_type=mesh_ids)
 
     lane = lax.broadcasted_iota(jnp.int32, (c1, 4 * c2), 1)
     for index, (pd, ph) in enumerate(phases):
-        for t, (td, th) in enumerate(taps):
+        for tap_index, (td, th) in enumerate(taps):
             tap = (3 - pd - 2 * td) * 4 + 3 - ph - 2 * th
             k = w_ref[:, tap * 4 * c2 : (tap + 1) * 4 * c2].astype(jnp.float32)
             down = pltpu.roll(k, 3 * c2, 1)
@@ -294,31 +282,42 @@
                 jnp.where(lane >= c2, up, 0.0),
                 jnp.where(lane >= 3 * c2, down, 0.0),
             ]
-            base = t * 4 * c1
+            base = tap_index * 4 * c1
             for j in range(4):
                 wide2[index, base + j * c1 : base + (j + 1) * c1, :] = blocks[j].astype(jnp.bfloat16)
 
-    none = jnp.zeros((c2, c3), jnp.bfloat16)
-    for t in range(16):
-        base = t * 6 * c2
-        k = [critic_ref[(4 * t + j) * c2 : (4 * t + j + 1) * c2, :] for j in range(4)]
-        left = [k[1], k[2], k[3], none, none, k[0]]
-        right = [none, k[0], k[1], k[2], k[3], none]
-        for j in range(6):
-            wide3[base + j * c2 : base + (j + 1) * c2, :c3] = left[j]
-            wide3[base + j * c2 : base + (j + 1) * c2, c3:] = right[j]
-
+    empty = jnp.zeros((cells, lanes), jnp.bfloat16)
+    for q in range(planes2):
+        hid[q, 0] = empty
+        hid[q, rows2 + 1] = empty
     blank = jnp.zeros((cells, 6 * c2), jnp.bfloat16)
     for d in range(img.shape[0]):
         img[d, 0, 0] = blank
         img[d, rows2, 1] = blank
 
-    for index, (pd, ph) in enumerate(phases):
+    def load(job):
+        for q in range(planes2):
+            pd, n = 1 - q % 2, q // 2
+            pair = jnp.stack([part_refs[(pd, 0)][job, n], part_refs[(pd, 1)][job, n]], axis=1)
+            hid[q, 1 : rows2 + 1] = pair.reshape(rows2, cells, lanes)
+
+        critic = critic_ref if job == 0 else mate_critic_ref
+        none = jnp.zeros((c2, c3), jnp.bfloat16)
+        for tap in range(16):
+            base = tap * 6 * c2
+            k = [critic[(4 * tap + j) * c2 : (4 * tap + j + 1) * c2, :] for j in range(4)]
+            at_left = [k[1], k[2], k[3], none, none, k[0]]
+            at_right = [none, k[0], k[1], k[2], k[3], none]
+            for j in range(6):
+                wide3[base + j * c2 : base + (j + 1) * c2, :c3] = at_left[j]
+                wide3[base + j * c2 : base + (j + 1) * c2, c3:] = at_right[j]
+
+    def generate(index):
+        pd, ph = phases[index]
         edge = 0 if pd == 1 else planes2 - 2
-        ends = low_end[0] if pd == 1 else high_end
-        inside = flags_ref[0] if pd == 1 else flags_ref[1]
-
-        def plane(n, carry, index=index, pd=pd, ph=ph, edge=edge, ends=ends, inside=inside):
+        inside = z > 0 if pd == 1 else z < lax.axis_size("depth") - 1
+
+        def plane(n, carry):
             parts = [
                 hid[n + td, th + ph : th + ph + rows2].reshape(rows2 * cells, lanes)
                 for td, th in taps
@@ -326,9 +325,7 @@
             total = jnp.dot(
                 jnp.concatenate(parts, axis=1), wide2[index], preferred_element_type=jnp.float32
             )
-            total = jnp.tanh(total)
-            if ends:
-                total = jnp.where(jnp.logical_or(n != edge, inside == 1), total, 0.0)
+            total = jnp.where(jnp.logical_or(n != edge, inside), jnp.tanh(total), 0.0)
             total = total.reshape(rows2, cells, 4 * c2)
             first, second = total[:, :, : 2 * c2], total[:, :, 2 * c2 :]
             place = lax.broadcasted_iota(jnp.int32, first.shape, 1)
@@ -336,72 +333,108 @@
             after = jnp.where(place == cells - 1, 0.0, pltpu.roll(first, cells - 1, 1))
             before = jnp.where(place == 0, 0.0, pltpu.roll(second, 1, 1))
             side = jnp.where(column < c2, after, before)
-            packed = jnp.concatenate([first, second, side], axis=2).astype(jnp.bfloat16)
+            result = jnp.concatenate([first, second, side], axis=2).astype(jnp.bfloat16)
             if ph == 0:
-                img[2 * n + 1 - pd, 0:rows2, 1] = packed
+                img[2 * n + 1 - pd, 0:rows2, 1] = result
             else:
-                img[2 * n + 1 - pd, 1 : rows2 + 1, 0] = packed
+                img[2 * n + 1 - pd, 1 : rows2 + 1, 0] = result
             return carry
 
         lax.fori_loop(0, planes2 - 1, plane, 0)
 
-    def judged(m, carry):
-        parts = [
-            img[2 * m + kd, kh // 2 : kh // 2 + rows2, kh % 2].reshape(rows2 * cells, 6 * c2)
-            for kd in range(4)
-            for kh in range(4)
-        ]
-        total = jnp.dot(
-            jnp.concatenate(parts, axis=1), wide3[...], preferred_element_type=jnp.float32
-        )
-        total = jnp.where(total > 0, total, leak_slope * total)
-        count = rows2 * cells
-        stage[pl.ds(0, count, stride=2), :] = total[:, :c3]
-        stage[pl.ds(1, count, stride=2), :] = total[:, c3:]
-        out_ref[m] = stage[...].reshape(rows2, 2 * cells, c3).astype(jnp.bfloat16)
-        return carry
-
-    lax.fori_loop(0, out_planes, judged, 0)
-
-
-def judged_planes(job, start, count, flags, parts, second, critic, name):
+    def judge(job):
+        def plane(m, carry):
+            parts = [
+                img[2 * m + kd, kh // 2 : kh // 2 + rows2, kh % 2].reshape(rows2 * cells, 6 * c2)
+                for kd in range(4)
+                for kh in range(4)
+            ]
+            total = jnp.dot(
+                jnp.concatenate(parts, axis=1), wide3[...], preferred_element_type=jnp.float32
+            )
+            total = jnp.where(total > 0, total, leak_slope * total)
+            count = rows2 * cells
+            stage[pl.ds(0, count, stride=2), :] = total[:, :c3]
+            stage[pl.ds(1, count, stride=2), :] = total[:, c3:]
+            out_ref[job, m] = stage[...].reshape(rows2, 2 * cells, c3).astype(jnp.bfloat16)
+            return carry
+
+        lax.fori_loop(0, out_planes, plane, 0)
+
+    half = out_planes // 2
+
+    def swap(r):
+        copies = []
+        for piece in (0, 1):
+            span = pl.ds(piece * half, half)
+            copy = pltpu.make_async_remote_copy(
+                src_ref=out_ref.at[1, span],
+                dst_ref=got.at[r, span],
+                send_sem=send_sem.at[piece, r],
+                recv_sem=recv_sem.at[piece, r],
+                device_id={"trainer": peers[bits[piece][r]]},
+                device_id_type=mesh_ids,
+            )
+            copy.start()
+            copies.append(copy)
+        return copies
+
+    def settle(r, copies):
+        for piece, copy in enumerate(copies):
+            copy.wait()
+            chosen = offset_ref[bits[piece][r]] == 1
+            for m in range(piece * half, (piece + 1) * half):
+                out_ref[1, m] = jnp.where(chosen, got[r, m], out_ref[1, m])
+
+    load(1)
+    for index in range(4):
+        generate(index)
+    judge(1)
+    pl.semaphore_wait(barrier, rounds)
+    moving = swap(0)
+    load(0)
+    settled = {(r + 1) * 4 // (rounds - 1) - 1: r for r in range(rounds - 1)}
+    for index in range(4):
+        generate(index)
+        if index in settled:
+            settle(settled[index], moving)
+            moving = swap(settled[index] + 1)
+    judge(0)
+    settle(rounds - 1, moving)
+
+
+def judged_both(offset_bits, parts, second, mate_critic, critic, bits):
     jobs, planes, rows, cells, lanes = parts[0].shape
-    total_planes = 2 * (planes - 1)
+    count = 2 * (planes - 1)
     rows2 = 2 * rows
+    c2 = second.shape[1] // 64
     c1 = second.shape[0]
-    c2 = second.shape[1] // 64
     c3 = critic.shape[1]
-    flops = 2 * rows2 * cells * 4 * c2 * ((count + 1) * 4 * 16 * c1 + count * 96 * c2)
-    part_spec = pl.BlockSpec((1, planes, rows, cells, lanes), lambda i: (job, 0, 0, 0, 0))
-    whole = lambda shape: pl.BlockSpec(shape, lambda i: (0,) * len(shape))
-    out_shape = (count, rows2, 2 * cells, c3)
+    rounds = len(bits[0])
+    flops = 2 * jobs * rows2 * cells * 4 * c2 * ((count + 1) * 4 * 16 * c1 + count * 96 * c2)
+    in_vmem = pl.BlockSpec(memory_space=pltpu.VMEM)
+    feature_shape = (count, rows2, 2 * cells, c3)
     return pl.pallas_call(
-        functools.partial(rest, (start == 0, start), start + count == total_planes),
-        grid=(1,),
-        out_shape=jax.ShapeDtypeStruct(out_shape, jnp.bfloat16),
-        in_specs=[
-            pl.BlockSpec(memory_space=pltpu.SMEM),
-            part_spec,
-            part_spec,
-            part_spec,
-            part_spec,
-            whole(second.shape),
-            whole(critic.shape),
-        ],
-        out_specs=whole(out_shape),
+        functools.partial(judged_kernel, bits),
+        out_shape=jax.ShapeDtypeStruct((jobs,) + feature_shape, jnp.bfloat16),
+        in_specs=[pl.BlockSpec(memory_space=pltpu.SMEM)] + [in_vmem] * 7,
+        out_specs=in_vmem,
         scratch_shapes=[
             pltpu.VMEM((count + 2, rows2 + 2, cells, lanes), jnp.bfloat16),
             pltpu.VMEM((4, 4 * lanes, 4 * c2), jnp.bfloat16),
             pltpu.VMEM((2 * count + 2, rows2 + 1, 2, cells, 6 * c2), jnp.bfloat16),
             pltpu.VMEM((96 * c2, 2 * c3), jnp.bfloat16),
             pltpu.VMEM((rows2 * cells * 2, c3), jnp.float32),
+            pltpu.VMEM((rounds,) + feature_shape, jnp.bfloat16),
+            pltpu.SemaphoreType.DMA((2, rounds)),
+            pltpu.SemaphoreType.DMA((2, rounds)),
         ],
-        compiler_params=pltpu.CompilerParams(vmem_limit_bytes=budget),
-        cost_estimate=pl.CostEstimate(
-            flops=flops, bytes_accessed=8 * parts[0].size, transcendentals=0
+        compiler_params=pltpu.CompilerParams(
+            vmem_limit_bytes=budget, collective_id=1, has_side_effects=True
         ),
-        name=name,
-    )(flags, *parts, second, critic)
+        cost_estimate=pl.CostEstimate(flops=flops, bytes_accessed=2**24, transcendentals=0),
+        name="judged",
+    )(offset_bits, *parts, second, mate_critic, critic)
 
 
 def local(latent, gen_first, gen_second, critic, partner):
@@ -412,27 +445,13 @@
         tuple(range(1, rounds)) + (0,),
         tuple(range(rounds - 1, 0, -1)) + (0,),
     )
-    z = lax.axis_index("depth")
-    flags = jnp.stack([z > 0, z < lax.axis_size("depth") - 1]).astype(jnp.int32)
-
     bits = orders[0]
     offset_bits = jnp.stack([jnp.bitwise_and(jnp.right_shift(offset, b), 1) for b in range(rounds)])
     *parts, second, mate_critic = hidden_parts(
         offset_bits, latent[0], gen_first[0], gen_second[0], critic[0], bits
     )
     second = second.reshape(-1, second.shape[2])
-    planes = 2 * latent.shape[1]
-    half = planes // 2
-    sent = judged_planes(1, 0, planes, flags, parts, second, mate_critic, "judged_mate")
-    received = [
-        exchanged(piece, offset, order)
-        for piece, order in zip((sent[:half], sent[half:]), orders)
-    ]
-    own = [
-        judged_planes(0, s, half, flags, parts, second, critic[0], "judged_own")
-        for s in (0, half)
-    ]
-    return jnp.stack([jnp.concatenate(own), jnp.concatenate(received)])[None]
+    return judged_both(offset_bits, parts, second, mate_critic, critic[0], orders)[None]
 
 
 def solution(mesh):

time: 208 us -> 189 us (0.909)
  waiting for transfers between devices: 10.2 us -> 0 us
  starting transfers between devices: 5.66 us -> 0 us
  other arithmetic: 4.24 us -> 0.56 us
    ppermute x6 -> x0, waiting for transfers between devices: 10.2 us -> none  [exchanged(): moved = lax.ppermute(value, 'trainer', pairs)]
    ppermute x6 -> x0, starting transfers between devices: 5.66 us -> none  [exchanged(): moved = lax.ppermute(value, 'trainer', pairs)]
    unnamed x4 -> x1, local copies, waits for them, and re-layouts: 0.01 us -> 3.27 us
    pallas_call x3 -> x1, Pallas kernels: 60.2 us -> 58.6 us  [judged_both(): pl.pallas_call(functools.partial(judged_kernel, bits), out_shape=jax.Shap...]
  transfers between devices with their start and end apart: 6 -> 0, of which waited for: 2 -> 0; matrix products, arithmetic and copies ran while one was open for 1% -> 0% of each run, Pallas kernels for 16% -> 0%
where the time goes in v3:
time: 189 us
  Pallas kernels  183 us (97%)
  local copies, waits for them, and re-layouts  4.51 us (2%)
    pallas_call x1, Pallas kernels, hidden_parts(): pl.pallas_call(functools.partial(hidden_kernel, bits), out_shape=[part] *...  124 us
    pallas_call x1, Pallas kernels, judged_both(): pl.pallas_call(functools.partial(judged_kernel, bits), out_shape=jax.Shap...  58.6 us

profile of v3, /device:TPU:0, one launch (start us, length us, event | category | flops | bytes accessed | tf_op | source)
XLA Modules:
  0.0 188.6 jit_solution(6112404135029260130)
XLA Ops:
  0.0 1.2 dynamic_slice.3
  1.9 0.6 pad_add_fusion.offset_ref
  2.5 124.2 %hidden.1 = (bf16[2,3,16,16,512]{4,3,2,1,0:T(8,128)(2,1)}, bf16[2,3,16,16,512]{4,3,2,1,0:T(8,128)(2,1)}, bf16[2,3,16,16,512]{4,3,2,1,0:T(8,128)(2,1)}, bf16[2,3,...) custom-call(s32[3]{0:T(128)} %pad_add_fusion.offset_ref, ...), custom_call_target="tpu_custom_call" | custom-call | flops 9663676416 | bytes 16777216 | tf_op jit(solution)/shard_map/hidden/pallas_call | solution.py:216
  126.6 58.6 %judged.1 = bf16[2,4,32,32,128]{4,3,2,1,0:T(8,128)(2,1)} custom-call(s32[3]{0:T(128)} %pad_add_fusion.offset_ref, bf16[2,3,16,16,512]{4,3,2,1,0:T(8,128)(2,1)} %get-tuple-element.11.p00, bf16[2,3,16,16,512]{4,3,2,1,0:T(8,128)(2,1)} %get-tuple-element.12.p01, bf16[2,3,16,16,512]{4,3,2,1,0:T(8,128)(2,1)} %get-tuple-element.13.p10, ...), custom_call_target="tpu_custom_call" | custom-call | flops 34359738368 | bytes 16777216 | tf_op jit(solution)/shard_map/judged/pallas_call | solution.py:417
  185.3 3.3 %copy.7 = bf16[1,2,4,32,32,128]{5,4,3,2,1,0:T(8,128)(2,1)} copy(bf16[1,2,4,32,32,128]{5,4,3,2,1,0:T(8,128)(2,1)} %bitcast.10) | data formatting | bytes 4194304

commit v4 on v3

--- a/solution.py
+++ b/solution.py
@@ -17,7 +17,7 @@
 def hidden_kernel(
     bits, offset_ref, lat_ref, first_ref, second_ref, critic_ref,
     p00, p01, p10, p11, second_out, critic_out,
-    first_buf, second_buf, lat_all, lat_cur, lat_got, critic_got, packed, wide, acc,
+    first_all, lat_all, lat_cur, lat_got, critic_got, packed, wide, acc,
     first_send, first_recv, second_send, second_recv,
     lat_send, lat_recv, critic_send, critic_recv, halo_send, halo_recv,
 ):
@@ -32,8 +32,8 @@
     towards = (right, left)
     peers = [t + (1 << b) * (1 - 2 * lax.rem(t // (1 << b), 2)) for b in bits]
     cs = first_ref.shape[0]
-    half = second_ref.shape[1] // 2
     quarter = first_ref.shape[1] // 4
+    last = count - 1
 
     barrier = pltpu.get_barrier_semaphore()
     for there in towards:
@@ -41,12 +41,12 @@
     for peer in peers:
         pl.semaphore_signal(barrier, inc=1, device_id={"trainer": peer}, device_id_type=mesh_ids)
 
-    for pd in (0, 1):
-        for td in (0, 1):
-            kd = 3 - pd - 2 * td
-            piece = first_ref[:, kd * quarter : (kd + 1) * quarter]
-            first_buf[pd, 0, td] = piece.astype(jnp.bfloat16)
-        second_buf[pd, 0] = second_ref[:, pd * half : (pd + 1) * half].astype(jnp.bfloat16)
+    for pd, td in taps:
+        for kh in range(4):
+            base = (3 - pd - 2 * td) * quarter + kh * 4 * c1
+            piece = first_ref[:, base : base + 4 * c1]
+            first_all[z, pd, td, kh] = piece.astype(jnp.bfloat16)
+    second_out[z] = second_ref[...].astype(jnp.bfloat16)
     lat_cur[...] = lat_ref[...]
     critic_out[...] = critic_ref[...]
     blank = jnp.zeros((cells, lat_ref.shape[3]), jnp.bfloat16)
@@ -66,29 +66,62 @@
         copy.start()
         return copy
 
-    def halo(job):
-        return [
-            sent(lat_all.at[job, slab], lat_all.at[job, 0], halo_send.at[job, 0],
-                 halo_recv.at[job, 0], depth=right),
-            sent(lat_all.at[job, 1], lat_all.at[job, slab + 1], halo_send.at[job, 1],
-                 halo_recv.at[job, 1], depth=left),
-        ]
-
-    def ring(step):
-        copies = []
-        for pd in (0, 1):
-            for td in (0, 1):
-                copies.append(
-                    sent(first_buf.at[pd, step, td], first_buf.at[pd, step + 1, td],
-                         first_send.at[pd, step, td], first_recv.at[pd, step, td],
-                         depth=towards[pd])
-                )
-        for pd in (0, 1):
-            copies.append(
-                sent(second_buf.at[pd, step], second_buf.at[pd, step + 1],
-                     second_send.at[pd, step], second_recv.at[pd, step], depth=towards[pd])
-            )
-        return copies
+    def halo(job, way):
+        src, dst = ((slab, 0), (1, slab + 1))[way]
+        return pltpu.make_async_remote_copy(
+            src_ref=lat_all.at[job, src], dst_ref=lat_all.at[job, dst],
+            send_sem=halo_send.at[job, way], recv_sem=halo_recv.at[job, way],
+            device_id={"depth": towards[way]}, device_id_type=mesh_ids,
+        )
+
+    def owner_of(way, step):
+        return lax.rem(z + count - step, count) if way == 0 else lax.rem(z + step, count)
+
+    def sends(way, step):
+        if way == 0:
+            return jnp.logical_and(z < last, z >= step - 1)
+        return jnp.logical_and(z > 0, z + step - 1 <= last)
+
+    def receives(way, step):
+        return z >= step if way == 0 else z + step <= last
+
+    def first_hop(way, step, owner, pd, td):
+        return pltpu.make_async_remote_copy(
+            src_ref=first_all.at[owner, pd, td], dst_ref=first_all.at[owner, pd, td],
+            send_sem=first_send.at[way, step - 1, pd, td],
+            recv_sem=first_recv.at[way, step - 1, pd, td],
+            device_id={"depth": towards[way]}, device_id_type=mesh_ids,
+        )
+
+    def second_hop(way, step, owner):
+        return pltpu.make_async_remote_copy(
+            src_ref=second_out.at[owner], dst_ref=second_out.at[owner],
+            send_sem=second_send.at[way, step - 1], recv_sem=second_recv.at[way, step - 1],
+            device_id={"depth": towards[way]}, device_id_type=mesh_ids,
+        )
+
+    def pass_first(step):
+        for pd, td in taps:
+            for way in (0, 1):
+                if step > 1:
+                    @pl.when(receives(way, step - 1))
+                    def _():
+                        first_hop(way, step - 1, owner_of(way, step - 1), pd, td).wait_recv()
+                if step < count:
+                    @pl.when(sends(way, step))
+                    def _():
+                        first_hop(way, step, owner_of(way, step - 1), pd, td).start()
+
+    def pass_second(step):
+        for way in (0, 1):
+            if step > 1:
+                @pl.when(receives(way, step - 1))
+                def _():
+                    second_hop(way, step - 1, owner_of(way, step - 1)).wait_recv()
+            if step < count:
+                @pl.when(sends(way, step))
+                def _():
+                    second_hop(way, step, owner_of(way, step - 1)).start()
 
     def swap_latent(r):
         return sent(lat_cur, lat_got.at[r], lat_send.at[r], lat_recv.at[r], trainer=peers[r])
@@ -100,9 +133,15 @@
     def chosen(r):
         return offset_ref[bits[r]] == 1
 
+    def start_halos(job):
+        for way in (0, 1):
+            @pl.when(sends(way, 1))
+            def _():
+                halo(job, way).start()
+
     moving = swap_latent(0)
-    halos = halo(0)
-    moves = ring(0)
+    start_halos(0)
+    pass_first(1)
     for r in range(len(bits)):
         moving.wait()
         lat_cur[...] = jnp.where(chosen(r), lat_got[r], lat_cur[...])
@@ -110,12 +149,18 @@
             moving = swap_latent(r + 1)
     for d in range(slab):
         lat_all[1, d + 1, 1 : rows + 1] = lat_cur[d]
-    halos += halo(1)
+    start_halos(1)
     critic_move = swap_critic(0)
-    for copy in halos:
-        copy.wait()
-    for end, inside in ((0, z > 0), (slab + 1, z < count - 1)):
-        lat_all[:, end] = jnp.where(inside, lat_all[:, end], jnp.zeros_like(lat_all[:, end]))
+    for way in (0, 1):
+        end = (0, slab + 1)[way]
+        for job in range(jobs):
+            @pl.when(receives(way, 1))
+            def _():
+                halo(job, way).wait_recv()
+
+            @pl.when(jnp.logical_not(receives(way, 1)))
+            def _():
+                lat_all[job, end] = jnp.zeros(lat_all.shape[2:], jnp.bfloat16)
 
     per = 128 // cs
     group_rows = jobs * (rows + 1)
@@ -147,42 +192,47 @@
     lax.fori_loop(0, planes, pack, 0)
 
     none = jnp.zeros((cs, c1), jnp.bfloat16)
+
+    def add_shard(owner, start):
+        def phase(index, carry):
+            pd, ph = index // 2, lax.rem(index, 2)
+            for td, th in taps:
+                block = first_all.at[owner, pd, td, 3 - ph - 2 * th]
+                k = [block[:, j * c1 : (j + 1) * c1] for j in range(4)]
+                for j, (a, b) in enumerate(((k[3], none), (k[1], k[2]), (none, k[0]))):
+                    base = (4 * j + 2 * td + th) * cs
+                    wide[base : base + cs, :c1] = a
+                    wide[base : base + cs, c1:] = b
+
+            def plane(n, inner):
+                lhs = packed[owner, :, n, pl.ds(ph, rows)].reshape(jobs * rows * cells, 12 * cs)
+                total = jnp.dot(lhs, wide[...], preferred_element_type=jnp.float32)
+                acc[index, n] = total if start else acc[index, n] + total
+                return inner
+
+            return lax.fori_loop(0, planes, plane, carry)
+
+        lax.fori_loop(0, 4, phase, 0)
+
     for step in range(count):
         if step:
-            for copy in moves:
-                copy.wait()
-            if step < count - 1:
-                moves = ring(step)
-        for pd in (0, 1):
-            owner = lax.rem(z + count - step, count) if pd == 0 else lax.rem(z + step, count)
-            second_out[owner, :, pd * half : (pd + 1) * half] = second_buf[pd, step]
-            for ph in (0, 1):
-                for td, th in taps:
-                    col = (3 - ph - 2 * th) * 4 * c1
-                    k = [
-                        first_buf[pd, step, td, :, col + j * c1 : col + (j + 1) * c1]
-                        for j in range(4)
-                    ]
-                    for j, (a, b) in enumerate(((k[3], none), (k[1], k[2]), (none, k[0]))):
-                        base = (4 * j + 2 * td + th) * cs
-                        wide[base : base + cs, :c1] = a
-                        wide[base : base + cs, c1:] = b
-
-                def plane(n, carry, ph=ph, index=2 * pd + ph, owner=owner, step=step):
-                    lhs = packed[owner, :, n, ph : ph + rows].reshape(
-                        jobs * rows * cells, 12 * cs
-                    )
-                    total = jnp.dot(lhs, wide[...], preferred_element_type=jnp.float32)
-                    acc[index, n] = total if step == 0 else acc[index, n] + total
-                    return carry
-
-                lax.fori_loop(0, planes, plane, 0)
+            pass_first(step + 1)
+        if step == min(2, last):
+            pass_second(1)
+        if step == 0:
+            add_shard(z, True)
+        else:
+            for way in (0, 1):
+                @pl.when(receives(way, step))
+                def _():
+                    add_shard(owner_of(way, step), False)
         if step < len(bits):
             critic_move.wait()
             critic_out[...] = jnp.where(chosen(step), critic_got[step], critic_out[...])
             if step + 1 < len(bits):
                 critic_move = swap_critic(step + 1)
 
+    pass_second(2)
     for index, (pd, ph) in enumerate(phases):
         edge = 0 if pd == 1 else planes - 1
         inside = z > 0 if pd == 1 else z < count - 1
@@ -200,6 +250,23 @@
             return carry
 
         lax.fori_loop(0, planes, finish, 0)
+        if index == 1:
+            pass_second(3)
+
+    for step in range(4, count + 1):
+        pass_second(step)
+    for way in (0, 1):
+        for step in range(1, count):
+            @pl.when(sends(way, step))
+            def _():
+                for pd, td in taps:
+                    first_hop(way, step, owner_of(way, step - 1), pd, td).wait_send()
+                second_hop(way, step, owner_of(way, step - 1)).wait_send()
+
+        @pl.when(sends(way, 1))
+        def _():
+            for job in range(jobs):
+                halo(job, way).wait_send()
 
 
 def hidden_parts(offset_bits, latent, first, second, critic, bits):
@@ -210,7 +277,6 @@
     rounds = len(bits)
     part = jax.ShapeDtypeStruct((2, slab + 1, rows, cells, 4 * c1), jnp.bfloat16)
     in_vmem = pl.BlockSpec(memory_space=pltpu.VMEM)
-    half = second.shape[1] // 2
     dma = pltpu.SemaphoreType.DMA
     flops = 2 * 2 * (slab + 1) * rows * cells * 4 * 12 * c0 * 2 * c1
     return pl.pallas_call(
@@ -223,8 +289,7 @@
         in_specs=[pl.BlockSpec(memory_space=pltpu.SMEM)] + [in_vmem] * 4,
         out_specs=[in_vmem] * 6,
         scratch_shapes=[
-            pltpu.VMEM((2, count, 2, cs, columns // 4), jnp.bfloat16),
-            pltpu.VMEM((2, count, second.shape[0], half), jnp.bfloat16),
+            pltpu.VMEM((count, 2, 2, 4, cs, columns // 16), jnp.bfloat16),
             pltpu.VMEM((2, slab + 2, rows + 2, cells, c0), jnp.bfloat16),
             pltpu.VMEM(latent.shape, jnp.bfloat16),
             pltpu.VMEM((rounds,) + latent.shape, jnp.bfloat16),
@@ -232,8 +297,8 @@
             pltpu.VMEM((count, 2, slab + 1, rows + 1, cells, 12 * cs), jnp.bfloat16),
             pltpu.VMEM((12 * cs, 2 * c1), jnp.bfloat16),
             pltpu.VMEM((4, slab + 1, 2 * rows * cells, 2 * c1), jnp.float32),
-            dma((2, count - 1, 2)),
-            dma((2, count - 1, 2)),
+            dma((2, count - 1, 2, 2)),
+            dma((2, count - 1, 2, 2)),
             dma((2, count - 1)),
             dma((2, count - 1)),
             dma((rounds,)),

time: 189 us -> 180 us (0.952)
  Pallas kernels: 183 us -> 175 us
    pallas_call x1, Pallas kernels: 124 us -> 114 us  [hidden_parts(): pl.pallas_call(functools.partial(hidden_kernel, bits), out_shape=[part] *...]
where the time goes in v4:
time: 180 us
  Pallas kernels  175 us (97%)
  local copies, waits for them, and re-layouts  4.51 us (3%)
    pallas_call x1, Pallas kernels, hidden_parts(): pl.pallas_call(functools.partial(hidden_kernel, bits), out_shape=[part] *...  114 us
    pallas_call x1, Pallas kernels, judged_both(): pl.pallas_call(functools.partial(judged_kernel, bits), out_shape=jax.Shap...  60.3 us

profile of v4, /device:TPU:0, one launch (start us, length us, event | category | flops | bytes accessed | tf_op | source)
XLA Modules:
  0.0 180.3 jit_solution(17616383993870325400)
XLA Ops:
  0.0 1.2 dynamic_slice.3
  1.9 0.6 pad_add_fusion.offset_ref
  2.5 114.2 %hidden.1 = (bf16[2,3,16,16,512]{4,3,2,1,0:T(8,128)(2,1)}, bf16[2,3,16,16,512]{4,3,2,1,0:T(8,128)(2,1)}, bf16[2,3,16,16,512]{4,3,2,1,0:T(8,128)(2,1)}, bf16[2,3,...) custom-call(s32[3]{0:T(128)} %pad_add_fusion.offset_ref, ...), custom_call_target="tpu_custom_call" | custom-call | flops 9663676416 | bytes 16777216 | tf_op jit(solution)/shard_map/hidden/pallas_call | solution.py:282
  116.7 60.3 %judged.1 = bf16[2,4,32,32,128]{4,3,2,1,0:T(8,128)(2,1)} custom-call(s32[3]{0:T(128)} %pad_add_fusion.offset_ref, bf16[2,3,16,16,512]{4,3,2,1,0:T(8,128)(2,1)} %get-tuple-element.11.p00, bf16[2,3,16,16,512]{4,3,2,1,0:T(8,128)(2,1)} %get-tuple-element.12.p01, bf16[2,3,16,16,512]{4,3,2,1,0:T(8,128)(2,1)} %get-tuple-element.13.p10, ...), custom_call_target="tpu_custom_call" | custom-call | flops 34359738368 | bytes 16777216 | tf_op jit(solution)/shard_map/judged/pallas_call | solution.py:482
  177.0 3.3 %copy.7 = bf16[1,2,4,32,32,128]{5,4,3,2,1,0:T(8,128)(2,1)} copy(bf16[1,2,4,32,32,128]{5,4,3,2,1,0:T(8,128)(2,1)} %bitcast.10) | data formatting | bytes 4194304

commit v5 on v4

--- a/solution.py
+++ b/solution.py
@@ -15,7 +15,7 @@
 
 
 def hidden_kernel(
-    bits, offset_ref, lat_ref, first_ref, second_ref, critic_ref,
+    bits, partner_ref, lat_ref, first_ref, second_ref, critic_ref,
     p00, p01, p10, p11, second_out, critic_out,
     first_all, lat_all, lat_cur, lat_got, critic_got, packed, wide, acc,
     first_send, first_recv, second_send, second_recv,
@@ -131,7 +131,7 @@
                     trainer=peers[r])
 
     def chosen(r):
-        return offset_ref[bits[r]] == 1
+        return jnp.bitwise_and(jnp.right_shift(partner_ref[0], bits[r]), 1) == 1
 
     def start_halos(job):
         for way in (0, 1):
@@ -269,7 +269,7 @@
                 halo(job, way).wait_send()
 
 
-def hidden_parts(offset_bits, latent, first, second, critic, bits):
+def hidden_parts(partner, latent, first, second, critic, bits):
     slab, rows, cells, c0 = latent.shape
     count = lax.axis_size("depth")
     cs, columns = first.shape
@@ -313,11 +313,11 @@
         ),
         cost_estimate=pl.CostEstimate(flops=flops, bytes_accessed=2**24, transcendentals=0),
         name="hidden",
-    )(offset_bits, latent, first, second, critic)
+    )(partner, latent, first, second, critic)
 
 
 def judged_kernel(
-    bits, offset_ref, p00, p01, p10, p11, w_ref, mate_critic_ref, critic_ref, out_ref,
+    bits, partner_ref, p00, p01, p10, p11, w_ref, mate_critic_ref, critic_ref, out_ref,
     hid, wide2, img, wide3, stage, got, send_sem, recv_sem,
 ):
     part_refs = {(0, 0): p00, (0, 1): p01, (1, 0): p10, (1, 1): p11}
@@ -390,7 +390,7 @@
             total = jnp.dot(
                 jnp.concatenate(parts, axis=1), wide2[index], preferred_element_type=jnp.float32
             )
-            total = jnp.where(jnp.logical_or(n != edge, inside), jnp.tanh(total), 0.0)
+            total = jnp.tanh(total)
             total = total.reshape(rows2, cells, 4 * c2)
             first, second = total[:, :, : 2 * c2], total[:, :, 2 * c2 :]
             place = lax.broadcasted_iota(jnp.int32, first.shape, 1)
@@ -405,7 +405,15 @@
                 img[2 * n + 1 - pd, 1 : rows2 + 1, 0] = result
             return carry
 
-        lax.fori_loop(0, planes2 - 1, plane, 0)
+        lax.fori_loop(0, planes2 - 1, plane, 0, unroll=True)
+
+        @pl.when(jnp.logical_not(inside))
+        def _():
+            outer = 2 * edge + 1 - pd
+            if ph == 0:
+                img[outer, 0:rows2, 1] = jnp.zeros((rows2,) + img.shape[3:], jnp.bfloat16)
+            else:
+                img[outer, 1 : rows2 + 1, 0] = jnp.zeros((rows2,) + img.shape[3:], jnp.bfloat16)
 
     def judge(job):
         def plane(m, carry):
@@ -447,7 +455,7 @@
     def settle(r, copies):
         for piece, copy in enumerate(copies):
             copy.wait()
-            chosen = offset_ref[bits[piece][r]] == 1
+            chosen = jnp.bitwise_and(jnp.right_shift(partner_ref[0], bits[piece][r]), 1) == 1
             for m in range(piece * half, (piece + 1) * half):
                 out_ref[1, m] = jnp.where(chosen, got[r, m], out_ref[1, m])
 
@@ -468,7 +476,7 @@
     settle(rounds - 1, moving)
 
 
-def judged_both(offset_bits, parts, second, mate_critic, critic, bits):
+def judged_both(partner, parts, second, mate_critic, critic, bits):
     jobs, planes, rows, cells, lanes = parts[0].shape
     count = 2 * (planes - 1)
     rows2 = 2 * rows
@@ -499,24 +507,21 @@
         ),
         cost_estimate=pl.CostEstimate(flops=flops, bytes_accessed=2**24, transcendentals=0),
         name="judged",
-    )(offset_bits, *parts, second, mate_critic, critic)
+    )(partner, *parts, second, mate_critic, critic)
 
 
 def local(latent, gen_first, gen_second, critic, partner):
-    trainer_index = lax.axis_index("trainer")
-    offset = jnp.bitwise_xor(partner[trainer_index], trainer_index)
     rounds = lax.axis_size("trainer").bit_length() - 1
     orders = (
         tuple(range(1, rounds)) + (0,),
         tuple(range(rounds - 1, 0, -1)) + (0,),
     )
     bits = orders[0]
-    offset_bits = jnp.stack([jnp.bitwise_and(jnp.right_shift(offset, b), 1) for b in range(rounds)])
     *parts, second, mate_critic = hidden_parts(
-        offset_bits, latent[0], gen_first[0], gen_second[0], critic[0], bits
+        partner, latent[0], gen_first[0], gen_second[0], critic[0], bits
     )
     second = second.reshape(-1, second.shape[2])
-    return judged_both(offset_bits, parts, second, mate_critic, critic[0], orders)[None]
+    return judged_both(partner, parts, second, mate_critic, critic[0], orders)[None]
 
 
 def solution(mesh):

time: 180 us -> 177 us (0.983)
  Pallas kernels: 175 us -> 173 us
where the time goes in v5:
time: 177 us
  Pallas kernels  173 us (98%)
  local copies, waits for them, and re-layouts  3.27 us (2%)
    pallas_call x1, Pallas kernels, hidden_parts(): pl.pallas_call(functools.partial(hidden_kernel, bits), out_shape=[part] *...  114 us
    pallas_call x1, Pallas kernels, judged_both(): pl.pallas_call(functools.partial(judged_kernel, bits), out_shape=jax.Shap...  59.2 us

profile of v5, /device:TPU:0, one launch (start us, length us, event | category | flops | bytes accessed | tf_op | source)
XLA Modules:
  0.0 176.7 jit_solution(12801157335641610661)
XLA Ops:
  0.0 114.2 %hidden.1 = (bf16[2,3,16,16,512]{4,3,2,1,0:T(8,128)(2,1)}, bf16[2,3,16,16,512]{4,3,2,1,0:T(8,128)(2,1)}, bf16[2,3,16,16,512]{4,3,2,1,0:T(8,128)(2,1)}, bf16[2,3,...) custom-call(s32[8]{0:T(128)} %partner_ref.3, ...), custom_call_target="tpu_custom_call" | custom-call | flops 9663676416 | bytes 16777216 | tf_op jit(solution)/shard_map/hidden/pallas_call | solution.py:282
  114.3 59.2 %judged.1 = bf16[2,4,32,32,128]{4,3,2,1,0:T(8,128)(2,1)} custom-call(s32[8]{0:T(128)} %partner_ref.3, bf16[2,3,16,16,512]{4,3,2,1,0:T(8,128)(2,1)} %get-tuple-element.11.p00, bf16[2,3,16,16,512]{4,3,2,1,0:T(8,128)(2,1)} %get-tuple-element.12.p01, bf16[2,3,16,16,512]{4,3,2,1,0:T(8,128)(2,1)} %get-tuple-element.13.p10, ...), custom_call_target="tpu_custom_call" | custom-call | flops 34359738368 | bytes 16777216 | tf_op jit(solution)/shard_map/judged/pallas_call | solution.py:490
  173.5 3.3 %copy.7 = bf16[1,2,4,32,32,128]{5,4,3,2,1,0:T(8,128)(2,1)} copy(bf16[1,2,4,32,32,128]{5,4,3,2,1,0:T(8,128)(2,1)} %bitcast.6) | data formatting | bytes 4194304
